TPU v7x, 128 devices: a whole 4x4x4 slice. The times are simulated.
128 devices in a mesh: row: 32 (over z, x, y_lo), feat: 4 (over y_hi, core).
Axes of the slice: x: 4, y: 4 (y_hi: 2, y_lo: 2; y = y_hi * 2 + y_lo), z: 4, core: 2. Of those that a mesh axis runs over, the one named last changes fastest.
Arguments:
- cells: bfloat16 [6144, 8, 192], P('row', 'feat'), may hold values from -16 to 16
- w_query: bfloat16 [192, 192], replicated, may hold values from -0.25 to 0.25
- w_key: bfloat16 [192, 192], replicated, may hold values from -0.25 to 0.25
- w_value: bfloat16 [192, 192], replicated, may hold values from -0.4375 to 0.4375
- w_out: bfloat16 [192, 192], replicated, may hold values from -0.4375 to 0.4375
- train_flag: int32 [6144], P('row'), may hold values from 0 to 1, as said below
- grad_out: bfloat16 [6144, 8, 192], P('row', 'feat'), may hold values from -6 to 6
Outputs:
- grad_cells: bfloat16 [6144, 8, 192], P('row', 'feat')
- grad_w_query: float32 [192, 192], replicated
- grad_w_key: float32 [192, 192], replicated
- grad_w_value: float32 [192, 192], replicated
- grad_w_out: float32 [192, 192], replicated
Inputs may be any that keep to these rules, and one draw needn't show every extreme that they name: train_flag is 1 on the first rows of the table and 0 on all later rows; at least 3072 rows are training rows and at least one row is a test row.
All inputs are finite; a program needn't handle non-finite values.
Results may differ from a plain program's by a relative error of at most 0.04.
The roundings to bfloat16 on the way count: a program that leaves them out, or rounds other values in their place, can miss the bound.
Values may be sent and summed in bfloat16 or wider, within the bound.
A program may use at most 128 MiB of HBM per device.

v0:
```python
import jax
import jax.numpy as jnp
from jax import lax
from jax.sharding import PartitionSpec as P

HEADS = 6


MASKED = -1e30


def block_size(length, stride_unit):
    chosen = stride_unit
    for factor in range(1, length // stride_unit + 1):
        if length % (stride_unit * factor) == 0 and stride_unit * factor <= 1024:
            chosen = stride_unit * factor
    return chosen


def piece_block(length):
    chosen = 1
    for candidate in range(1, min(length, 1024) + 1):
        if length % candidate == 0:
            chosen = candidate
    return chosen


def masked_scores(queries, keys_block, flags_block, score_scale):
    scores = (
        jnp.einsum("qfhd,kfhd->fhqk", queries, keys_block, preferred_element_type=jnp.float32)
        * score_scale
    )
    return jnp.where(flags_block[None, None, None, :] > 0.5, scores, MASKED)


def probability(scores, maxima, totals):
    return jnp.exp(scores - maxima[..., None]) / totals[..., None]


def body(cells, w_query, w_key, w_value, w_out, train_flag, grad_out):
    row_count, feat_count, model_width = cells.shape
    head_count = HEADS
    head_size = model_width // head_count
    score_scale = float(head_size) ** (-0.5)
    shape_four = (row_count, feat_count, head_count, head_size)
    flat_cells = cells.reshape(-1, model_width)
    flat_grad = grad_out.reshape(-1, model_width)
    query = jnp.dot(flat_cells, w_query, preferred_element_type=jnp.float32).astype(jnp.bfloat16)
    key_flat = jnp.dot(flat_cells, w_key, preferred_element_type=jnp.float32).astype(jnp.bfloat16)
    value_flat = jnp.dot(flat_cells, w_value, preferred_element_type=jnp.float32).astype(
        jnp.bfloat16
    )
    query_four = query.reshape(shape_four)
    flag_float = train_flag.astype(jnp.bfloat16)
    key_all, value_all, flag_all = (
        lax.all_gather(
            key_flat.reshape(row_count, feat_count, model_width), "row", axis=0, tiled=True
        ),
        lax.all_gather(
            value_flat.reshape(row_count, feat_count, model_width), "row", axis=0, tiled=True
        ),
        lax.all_gather(flag_float, "row", axis=0, tiled=True),
    )
    all_rows = key_all.shape[0]
    stride = block_size(all_rows, row_count)
    block_count = all_rows // stride

    def key_block(begin, length):
        keys_block = lax.dynamic_slice_in_dim(key_all, begin, length, 0).reshape(
            length, feat_count, head_count, head_size
        )
        values_block = lax.dynamic_slice_in_dim(value_all, begin, length, 0).reshape(
            length, feat_count, head_count, head_size
        )
        flags_block = lax.dynamic_slice_in_dim(flag_all, begin, length, 0)
        return (keys_block, values_block, flags_block)

    def stats_step(index, carry):
        maxima, totals = carry
        keys_block, values_block, flags_block = key_block(index * stride, stride)
        scores = masked_scores(query_four, keys_block, flags_block, score_scale)
        newmax = jnp.maximum(maxima, jnp.max(scores, axis=-1))
        totals = totals * jnp.exp(maxima - newmax) + jnp.sum(
            jnp.exp(scores - newmax[..., None]), axis=-1
        )
        return (newmax, totals)

    stat_shape = (feat_count, head_count, row_count)
    maxima, totals = lax.fori_loop(
        0,
        block_count,
        stats_step,
        (jnp.full(stat_shape, MASKED, jnp.float32), jnp.zeros(stat_shape, jnp.float32)),
    )

    def output_step(index, accum):
        keys_block, values_block, flags_block = key_block(index * stride, stride)
        attention = probability(
            masked_scores(query_four, keys_block, flags_block, score_scale), maxima, totals
        ).astype(jnp.bfloat16)
        return accum + jnp.einsum(
            "fhqk,kfhd->fhqd", attention, values_block, preferred_element_type=jnp.float32
        )

    accum_shape = (feat_count, head_count, row_count, head_size)
    attended_heads = lax.fori_loop(
        0, block_count, output_step, jnp.zeros(accum_shape, jnp.float32)
    ).astype(jnp.bfloat16)
    attended_four = attended_heads.transpose(2, 0, 1, 3)
    attended_flat = attended_four.reshape(-1, model_width)
    grad_attended = jnp.dot(flat_grad, w_out.T, preferred_element_type=jnp.float32).astype(
        jnp.bfloat16
    )
    grad_four = grad_attended.reshape(shape_four)
    delta_rows = jnp.sum(grad_four.astype(jnp.float32) * attended_four.astype(jnp.float32), axis=-1)
    delta = delta_rows.transpose(1, 2, 0)

    def query_step(index, accum):
        keys_block, values_block, flags_block = key_block(index * stride, stride)
        attention = probability(
            masked_scores(query_four, keys_block, flags_block, score_scale), maxima, totals
        )
        grad_attention = jnp.einsum(
            "qfhd,kfhd->fhqk", grad_four, values_block, preferred_element_type=jnp.float32
        )
        grad_scores = (attention * (grad_attention - delta[..., None]) * score_scale).astype(
            jnp.bfloat16
        )
        return accum + jnp.einsum(
            "fhqk,kfhd->fhqd", grad_scores, keys_block, preferred_element_type=jnp.float32
        )

    grad_q_heads = lax.fori_loop(
        0, block_count, query_step, jnp.zeros(accum_shape, jnp.float32)
    ).astype(jnp.bfloat16)
    grad_query = grad_q_heads.transpose(2, 0, 1, 3).reshape(-1, model_width)
    offset = jnp.int32(0)
    amount = lax.axis_size("row") * row_count
    inner = piece_block(amount)

    def one_block(index, buffer):
        keys_block, values_block, flags_block = key_block(offset + index * inner, inner)
        attention = probability(
            masked_scores(query_four, keys_block, flags_block, score_scale), maxima, totals
        )
        attention_b = attention.astype(jnp.bfloat16)
        grad_attention = jnp.einsum(
            "qfhd,kfhd->fhqk", grad_four, values_block, preferred_element_type=jnp.float32
        )
        grad_scores = (attention * (grad_attention - delta[..., None]) * score_scale).astype(
            jnp.bfloat16
        )
        grad_k = jnp.einsum(
            "fhqk,qfhd->kfhd", grad_scores, query_four, preferred_element_type=jnp.float32
        )
        grad_v = jnp.einsum(
            "fhqk,qfhd->kfhd", attention_b, grad_four, preferred_element_type=jnp.float32
        )
        both = jnp.stack(
            [
                grad_k.reshape(inner, feat_count, model_width),
                grad_v.reshape(inner, feat_count, model_width),
            ],
            1,
        )
        return lax.dynamic_update_slice_in_dim(buffer, both, index * inner, 0)

    start_buffer = jnp.zeros((amount, 2, feat_count, model_width), jnp.float32)
    key_grads = lax.psum_scatter(
        lax.fori_loop(0, amount // inner, one_block, start_buffer),
        "row",
        scatter_dimension=0,
        tiled=True,
    )
    grad_key = key_grads[:, 0].astype(jnp.bfloat16).reshape(-1, model_width)
    grad_value = key_grads[:, 1].astype(jnp.bfloat16).reshape(-1, model_width)
    contract = (((0,), (0,)), ((), ()))
    part_out = lax.dot_general(
        attended_flat, flat_grad, contract, preferred_element_type=jnp.float32
    )
    part_query = lax.dot_general(
        flat_cells, grad_query, contract, preferred_element_type=jnp.float32
    )
    part_key = lax.dot_general(flat_cells, grad_key, contract, preferred_element_type=jnp.float32)
    part_value = lax.dot_general(
        flat_cells, grad_value, contract, preferred_element_type=jnp.float32
    )
    grad_w_query, grad_w_key, grad_w_value, grad_w_out = lax.psum(
        (part_query, part_key, part_value, part_out), ("row", "feat")
    )
    summed = flat_grad.astype(jnp.float32)
    summed = summed + jnp.dot(grad_query, w_query.T, preferred_element_type=jnp.float32)
    summed = summed + jnp.dot(grad_key, w_key.T, preferred_element_type=jnp.float32)
    summed = summed + jnp.dot(grad_value, w_value.T, preferred_element_type=jnp.float32)
    grad_cells = summed.astype(jnp.bfloat16).reshape(row_count, feat_count, model_width)
    return (grad_cells, grad_w_query, grad_w_key, grad_w_value, grad_w_out)


def solution(mesh):
    return jax.shard_map(
        body,
        mesh=mesh,
        in_specs=(P("row", "feat", None), P(), P(), P(), P(), P("row"), P("row", "feat", None)),
        out_specs=(P("row", "feat", None), P(), P(), P(), P()),
        check_vma=False,
    )
```

profile of v0, /device:TPU:25, one launch (start us, length us, event | category | flops | bytes accessed | tf_op | source)
XLA Modules:
  0.0 1116.7 jit_solution(18123216632321591599)
XLA Ops:
  16.9 131.9 %all-reduce = bf16[6144]{0:T(1024)(128)(2,1)S(1)} all-reduce(bf16[6144]{0:T(1024)(128)(2,1)S(1)} %dynamic-update-slice), channel_id=1, replica_groups=mesh['row'=32,'feat'=4] {'row'}, use_global_device_ids=true, to_apply=%add | all-reduce | flops 6144 | bytes 24576
  152.3 8.9 all-gather.3.cloned.1.call-done
  161.2 15.9 %copy.97 = bf16[6144,2,192]{0,2,1:T(8,128)(2,1)} copy(bf16[6144,2,192]{2,1,0:T(2,128)(2,1)} %all-gather.3.cloned.1.call-done) | data formatting | bytes 9437184
  177.1 75.2 %while.58 = (s32[]{:T(128)}, f32[2,6,192]{2,1,0:T(8,128)S(1)}, f32[2,6,192]{2,1,0:T(8,128)S(1)}, bf16[6144]{0:T(1024)(128)(2,1)S(1)}, bf16[6144,2,192]{0,2,1:T(8...) while((s32[]{:T(128)}, f32[2,6,192]{2,1,0:T(8,128)S(1)}, ...), condition=%wide.region_3.4_spmd.clone, body=%wide.region_0.3_spmd.clone.sunk | while | flops 125646344 | bytes 16196518 | solution.py:89
  252.3 74.5 %all-gather.5.cloned.1.call-done = bf16[6144,2,192]{2,1,0:T(2,128)(2,1)} async-done(((bf16[192,2,192]{2,1,0:T(2,128)(2,1)}), bf16[6144,2,192]{2,1,0:T(2,128)(2,1)}) %all-gather.5.cloned.1.call-update) | async-done | bytes 4718608 | tf_op jit(solution)/shard_map/all_gather | solution.py:59
  326.8 15.9 %copy.99 = bf16[6144,2,192]{0,2,1:T(8,128)(2,1)} copy(bf16[6144,2,192]{2,1,0:T(2,128)(2,1)} %all-gather.5.cloned.1.call-done) | data formatting | bytes 9437184
  342.7 38.3 %while.59 = (s32[]{:T(128)}, f32[2,6,192,32]{2,3,1,0:T(8,128)S(1)}, bf16[6144]{0:T(1024)(128)(2,1)S(1)}, bf16[6144,2,192]{0,2,1:T(8,128)(2,1)}, bf16[192,2,6,32]...) while((s32[]{:T(128)}, f32[2,6,192,32]{2,3,1,0:T(8,128)S(1)}, ...), condition=%wide.region_5.6_spmd.clone, body=%wide.region_4.5_spmd.clone.sunk | while | flops 235489536 | bytes 4297909 | solution.py:106
  382.0 8.8 broadcast_in_dim.138
  390.9 117.1 %while.57 = (s32[]{:T(128)}, f32[6144,2,2,192]{0,3,2,1:T(8,128)}, bf16[6144]{0:T(1024)(128)(2,1)S(1)}, bf16[6144,2,192]{0,2,1:T(8,128)(2,1)}, bf16[192,2,6,32]{0...) while((s32[]{:T(128)}, f32[6144,2,2,192]{0,3,2,1:T(8,128)}, ...), condition=%wide.region_10.11_spmd, body=%wide.region_9.10_spmd.sunk | while | flops 626002944 | bytes 43089084 | solution.py:170
  397.5 6.3 fusion.97
  475.6 6.3 fusion.97
  495.1 6.3 fusion.97
  508.0 18.6 %copy.119 = f32[6144,768]{1,0:T(8,128)} copy(f32[6144,768]{0,1:T(8,128)} %bitcast.141) | data formatting | bytes 37748736
  527.7 95.1 %while.60 = (s32[]{:T(128)}, f32[2,6,192,32]{2,3,1,0:T(8,128)S(1)}, bf16[6144]{0:T(1024)(128)(2,1)S(1)}, bf16[6144,2,192]{0,2,1:T(8,128)(2,1)}, bf16[192,2,6,32]...) while((s32[]{:T(128)}, f32[2,6,192,32]{2,3,1,0:T(8,128)S(1)}, ...), condition=%wide.region_8.9_spmd.clone, body=%wide.region_7.8_spmd.clone.sunk | while | flops 354044160 | bytes 19200196 | solution.py:133
  533.3 6.4 fusion.112
  545.1 6.4 fusion.112
  557.0 6.4 fusion.112
  568.9 6.4 fusion.112
  580.7 6.5 fusion.112
  592.7 6.4 fusion.112
  604.5 6.4 fusion.112
  616.4 6.4 fusion.112
  627.3 322.0 %reduce-scatter.4.cloned.1.call-done = f32[192,768]{1,0:T(8,128)} async-done(((f32[6144,768]{1,0:T(8,128)}), f32[192,768]{1,0:T(8,128)}) %reduce-scatter.4.cloned.1.call-update) | async-done | bytes 589840
  954.6 148.8 %all-reduce.4.cloned.1.call-done = (f32[192,192]{0,1:T(8,128)}, f32[192,192]{0,1:T(8,128)}, f32[192,192]{0,1:T(8,128)}, f32[192,192]{1,0:T(8,128)}) async-done(((f32[192,192]{0,1:T(8,128)}, f32[192,192]{0,1:T(8,128)}, f32[192,192]{0,1:T(8,128)}, f32[192,192]{1,0:T(8,128)}), (f32[192,192]{0,1:T(8,128)}, f32[192,192]{0,1:T(8,128)}, f32[192,192]{0,1:T(8,128)}, ...) | async-done | bytes 589840 | tf_op jit(solution)/shard_map/psum | solution.py:188
  (215 shorter events, 285.5 us)
Async XLA Ops:
  7.2 5.6 copy-start
  7.2 154.0 %all-gather.3.cloned.1.call-start = ((), (), s32[]{:S(2)}) async-start(), calls=%async_computation.1 | async-start | bytes 6488064 | tf_op jit(solution)/shard_map/all_gather | solution.py:56
  8.3 168.8 %copy-start.1 = (bf16[384,192]{1,0:T(8,128)(2,1)}, bf16[384,192]{1,0:T(8,128)(2,1)S(1)}, u32[]{:S(2)}) copy-start(bf16[384,192]{1,0:T(8,128)(2,1)S(1)} %reshape.126) | copy-start | bytes 442372
  10.5 316.3 %all-gather.5.cloned.1.call-start = ((), (), s32[]{:S(2)}) async-start(), calls=%async_computation.2 | async-start | bytes 6488064 | tf_op jit(solution)/shard_map/all_gather | solution.py:59
  12.7 936.6 %reduce-scatter.4.cloned.1.call-start = ((), (), s32[]{:S(2)}) async-start(), calls=%async_computation.3 | async-start | bytes 19464192
  150.0 27.1 %copy-start.3 = (bf16[384,192]{1,0:T(8,128)(2,1)}, bf16[384,192]{1,0:T(8,128)(2,1)S(1)}, u32[]{:S(2)}) copy-start(bf16[384,192]{1,0:T(8,128)(2,1)S(1)} %reshape.125) | copy-start | bytes 442372
  526.6 0.9 copy-start.4
  526.7 576.7 %all-reduce.4.cloned.1.call-start = ((), (), s32[]{:S(2)}) async-start(), calls=%async_computation.4 | async-start | bytes 1572864 | tf_op jit(solution)/shard_map/psum | solution.py:188
  527.7 96.4 %copy-start.6 = (bf16[192,2,6,32]{0,3,2,1:T(8,128)(2,1)S(1)}, bf16[192,2,6,32]{0,3,2,1:T(8,128)(2,1)}, u32[]{:S(2)}) copy-start(bf16[192,2,6,32]{0,3,2,1:T(8,128)(2,1)} %get-tuple-element.907) | copy-start | bytes 442372
  527.7 97.5 %copy-start.2 = (bf16[384,192]{1,0:T(8,128)(2,1)S(1)}, bf16[384,192]{1,0:T(8,128)(2,1)}, u32[]{:S(2)}) copy-start(bf16[384,192]{1,0:T(8,128)(2,1)} %copy-done.1) | copy-start | bytes 442372
  622.9 327.7 %copy-start.5 = (bf16[192,2,192]{2,1,0:T(2,128)(2,1)S(1)}, bf16[192,2,192]{2,1,0:T(2,128)(2,1)}, u32[]{:S(2)}) copy-start(bf16[192,2,192]{2,1,0:T(2,128)(2,1)} %param.15) | copy-start | bytes 442372
  622.9 329.9 %copy-start.7 = (bf16[192,192]{1,0:T(8,128)(2,1)S(1)}, bf16[192,192]{1,0:T(8,128)(2,1)}, u32[]{:S(2)}) copy-start(bf16[192,192]{1,0:T(8,128)(2,1)} %param.17) | copy-start | bytes 221188
  622.9 330.5 %copy-start.8 = (bf16[192,192]{1,0:T(8,128)(2,1)S(1)}, bf16[192,192]{1,0:T(8,128)(2,1)}, u32[]{:S(2)}) copy-start(bf16[192,192]{1,0:T(8,128)(2,1)} %param.18) | copy-start | bytes 221188
Sparse Core Ops, SparseCore 0:
  10.7 150.4 all-gather.2
  163.4 163.3 all-gather.4
  526.8 422.4 reduce-scatter.3
  954.8 148.4 all-reduce.3
where the time goes:
time: 1120 us
  waiting for transfers between devices  554 us (49%)
  matrix products  248 us (22%)
  blocking collectives  132 us (12%)
  local copies, waits for them, and re-layouts  119 us (11%)
  other arithmetic  47.6 us (4%)
  between operations  14.8 us (1%)
    unnamed x5, waiting for transfers between devices  322 us
    psum x1, waiting for transfers between devices, body(): lax.psum((part_query, part_key, part_value, part_out), ('row', 'feat'))  149 us
    unnamed x1, blocking collectives  132 us
    dot_general x22, matrix products, masked_scores(): jnp.einsum('qfhd,kfhd->fhqk', queries, keys_block, preferred_element_type...  95.8 us
    all_gather x1, waiting for transfers between devices, body(): lax.all_gather(value_flat.reshape(row_count, feat_count, model_width), 'r...  74.5 us
    unnamed x33, local copies, waits for them, and re-layouts  62.1 us
    dot_general x8, matrix products, query_step(): jnp.einsum('fhqk,kfhd->fhqd', grad_scores, keys_block, preferred_element_...  51.2 us
    dot_general x6, matrix products, one_block(): jnp.einsum('fhqk,qfhd->kfhd', grad_scores, query_four, preferred_element_...  37.8 us
  transfers between devices with their start and end apart: 4, of which 4 were waited for; matrix products, arithmetic and copies ran while one was open for 18% of the time, Pallas kernels for 0%

commit v1 on v0

v1 whole, which is shorter than its diff:
```python
import functools

import jax
import jax.numpy as jnp
from jax import lax
from jax.experimental import pallas as pl
from jax.experimental.pallas import tpu as pltpu
from jax.sharding import PartitionSpec as P


HD = 32
SCALE = float(HD) ** -0.5
SCALE_LOG2E = SCALE * 1.4426950408889634
BIAS = -1e30
F32 = jnp.float32
BF = jnp.bfloat16
MESH = pl.DeviceIdType.MESH

E = 192
HALF = 96
ROWS = 192
NQ = 768
NR = 6144
KC = 1024


def dot(a, b):
    return jnp.dot(a, b, preferred_element_type=F32)


def dot_t(a, b):
    return lax.dot_general(a, b, (((1,), (1,)), ((), ())), preferred_element_type=F32)


def t_dot(a, b):
    return lax.dot_general(a, b, (((0,), (0,)), ((), ())), preferred_element_type=F32)


def place():
    row = lax.axis_index("row")
    feat = lax.axis_index("feat")
    return row // 8, (row // 2) % 4, row % 2, feat // 2, feat % 2


def device(z, x, yl, yh, c):
    return ((z * 4 + x) * 2 + yl, yh * 2 + c)


def iotas(shape):
    return lax.broadcasted_iota(jnp.int32, shape, 0), lax.broadcasted_iota(jnp.int32, shape, 1)


def pick_rows(f):
    i, j = iotas((ROWS, 2 * ROWS))
    return (j == 2 * i + f).astype(F32).astype(BF)


def spread_lanes():
    i, j = iotas((E, 256))
    return (j == i + jnp.where(i >= HALF, 128 - HALF, 0)).astype(F32).astype(BF)


def rcopy(src, dst, send, recv, to):
    return pltpu.make_async_remote_copy(
        src_ref=src, dst_ref=dst, send_sem=send, recv_sem=recv, device_id=to, device_id_type=MESH
    )


def share_kernel(cells_ref, grad_ref, wq_ref, wk_ref, wv_ref, wo_ref, flag_ref, kv_ref, qg_ref,
                 kvs, qgs, s1, r1, s2, r2, zs, zr, fs, fr, cs, cr):
    z, x, yl, yh, c = place()
    mine = x // 2 == c
    own = jnp.where(mine, 1, 0)
    zp, zn = (z + 1) % 4, (z + 3) % 4
    up, down, twin = device(zp, x, yl, yh, c), device(zn, x, yl, yh, c), device(z, x, yl, yh, 1 - c)
    slot = (x % 2) * 2 + yl

    barrier = pltpu.get_barrier_semaphore()
    for to in (up, down, twin):
        pl.semaphore_signal(barrier, inc=1, device_id=to, device_id_type=MESH)
    for s in range(4):
        @pl.when(jnp.logical_not(jnp.logical_and(mine, slot == s)))
        def _():
            pl.semaphore_signal(
                barrier, inc=1, device_id=device(z, 2 * c + s // 2, s % 2, yh, x // 2), device_id_type=MESH
            )

    spread = spread_lanes()
    lane = lax.broadcasted_iota(jnp.int32, (ROWS, 128), 1)
    k_extra = jnp.where((lane == HALF) & (flag_ref[...] <= 0), BIAS, 0.0)
    v_extra = jnp.where((lane >= HALF) & (lane < HALF + 3), 1.0, 0.0)
    cells = cells_ref[...]
    grad = grad_ref[...]
    for f in range(2):
        pick = pick_rows(f)
        cf = dot(pick, cells).astype(BF)
        gf = dot(pick, grad).astype(BF)
        k = dot(dot(cf, wk_ref[...]).astype(BF), spread)
        v = dot(dot(cf, wv_ref[...]).astype(BF), spread)
        q = dot(dot(cf, wq_ref[...]).astype(BF), spread)
        g = dot(dot_t(gf, wo_ref[...]).astype(BF), spread)
        for h in range(2):
            a = slice(128 * h, 128 * h + 128)
            kvs[2 * f + h, :, 0:128] = (k[:, a] + k_extra).astype(BF)
            kvs[2 * f + h, :, 128:256] = (v[:, a] + v_extra).astype(BF)
            qgs[2 * f + h, :, 0:128] = q[:, a].astype(BF)
            qgs[2 * f + h, :, 128:256] = g[:, a].astype(BF)

    pl.semaphore_wait(barrier, 7 - own)

    my_rows = pl.ds(pl.multiple_of(z * 1536 + x * 384 + yl * 192, 192), 192)
    my_slot = pl.ds(pl.multiple_of(slot * 192, 192), 192)

    def first(j):
        to = device(z, 2 * c + j // 2, j % 2, yh, x // 2)
        a = rcopy(kvs.at[j], kv_ref.at[my_rows, :], s1.at[j], r1.at[slot], to)
        b = rcopy(qgs.at[j], qg_ref.at[my_slot, :], s2.at[j], r2.at[slot], to)
        return a, b

    for j in range(4):
        keep = jnp.logical_and(mine, slot == j)

        @pl.when(keep)
        def _():
            pltpu.make_async_copy(kvs.at[j], kv_ref.at[my_rows, :], r1.at[slot]).start()
            pltpu.make_async_copy(qgs.at[j], qg_ref.at[my_slot, :], r2.at[slot]).start()

        @pl.when(jnp.logical_not(keep))
        def _():
            a, b = first(j)
            a.start()
            b.start()

    def rows_of(zz, cc, s):
        return pl.ds(pl.multiple_of(zz * 1536 + cc * 768 + s * 192, 192), 192)

    def move(zz, s, send, recv, to):
        r = rows_of(zz, c, s)
        return rcopy(kv_ref.at[r, :], kv_ref.at[r, :], send, recv, to)

    def landed(zz, cc, s, recv):
        r = rows_of(zz, cc, s)
        pltpu.make_async_copy(kv_ref.at[r, :], kv_ref.at[r, :], recv).wait()

    sent = []

    def go(copy):
        copy.start()
        sent.append(copy)

    for s in range(4):
        landed(z, c, s, r1.at[s])
        go(move(z, s, zs.at[s], zr.at[s], up))
        go(move(z, s, zs.at[4 + s], zr.at[4 + s], down))
        go(move(z, s, cs.at[s], cr.at[s], twin))
    for i in range(4):
        s = i
        landed(zn, c, s, zr.at[s])
        if s < 2:
            go(move(zn, s, fs.at[s], fr.at[s], up))
        go(move(zn, s, cs.at[4 + s], cr.at[4 + s], twin))
        s = (i + 2) % 4
        landed(zp, c, s, zr.at[4 + s])
        if s >= 2:
            go(move(zp, s, fs.at[s], fr.at[s], down))
        go(move(zp, s, cs.at[8 + s], cr.at[8 + s], twin))
    zo = (z + 2) % 4
    for s in (0, 2, 1, 3):
        landed(zo, c, s, fr.at[s])
        go(move(zo, s, cs.at[12 + s], cr.at[12 + s], twin))
    for n, zz in ((0, z), (1, zn), (2, zp), (3, zo)):
        for s in range(4):
            landed(zz, 1 - c, s, cr.at[4 * n + s])
    for s in range(4):
        q = pl.ds(s * 192, 192)
        pltpu.make_async_copy(qg_ref.at[q, :], qg_ref.at[q, :], r2.at[s]).wait()
    for copy in sent:
        copy.wait_send()
    for j in range(4):
        @pl.when(jnp.logical_not(jnp.logical_and(mine, slot == j)))
        def _():
            a, b = first(j)
            a.wait_send()
            b.wait_send()


def attention_kernel(kv_ref, qg_ref, dkv_ref, qa_ref, e_ref, mb_ref, kT_ref, vT_ref, qT_ref, gT_ref, qm_ref, gm_ref,
                     qmT_ref, gmT_ref, acc_ref, m_ref, dkv_acc, attT_ref, dqT_ref):
    lane = lax.broadcasted_iota(jnp.int32, (1, 128), 1)

    def rows(c):
        return pl.ds(pl.multiple_of(c * KC, KC), KC)

    def count(c, total):
        kept = jnp.where(kv_ref[rows(c), 0:128].astype(F32) > 0.5 * BIAS, 1.0, 0.0)
        return total + jnp.sum(kept, axis=0, keepdims=True)

    kept = lax.fori_loop(0, NR // KC, count, jnp.zeros((1, 128), F32))
    train = jnp.sum(jnp.where(lane == HALF, kept, 0.0)).astype(jnp.int32)
    nk = lax.div(train + KC - 1, KC)

    @pl.loop(nk, NR // KC)
    def _(c):
        dkv_ref[rows(c), :] = jnp.zeros((KC, 256), BF)

    @pl.loop(0, nk)
    def _(c):
        r = rows(c)
        kT_ref[:, r] = kv_ref[r, 0:128].T
        vT_ref[:, r] = kv_ref[r, 128:256].T

    qT_ref[...] = qg_ref[:, 0:128].T
    gT_ref[...] = qg_ref[:, 128:256].T
    attT_ref[...] = jnp.zeros_like(attT_ref)
    dqT_ref[...] = jnp.zeros_like(dqT_ref)
    i16 = lax.broadcasted_iota(jnp.int32, (16, NQ), 0)

    for h in range(3):
        hs = slice(32 * h, 32 * h + 32)
        qmT_ref[...] = jnp.zeros_like(qmT_ref)
        qmT_ref[hs, :] = qT_ref[hs, :]
        qm_ref[...] = qmT_ref[...].T
        qmT_ref[96:112, :] = jnp.where(i16 == 0, 1.0, 0.0).astype(BF)
        acc_ref[...] = jnp.zeros_like(acc_ref)
        m_ref[...] = jnp.full_like(m_ref, BIAS)

        @pl.loop(0, nk)
        def _(c):
            r = rows(c)
            vt = jnp.concatenate([vT_ref[hs, r], vT_ref[96:112, r]], 0)
            s = dot(kv_ref[r, 0:128], qmT_ref[...]) * SCALE_LOG2E
            old = m_ref[0:1, :]
            new = jnp.maximum(old, jnp.ceil(jnp.max(s, axis=0, keepdims=True)))
            e = jnp.exp2(s - new).astype(BF)
            e_ref[r, :] = e
            m_ref[0:1, :] = new
            mb_ref[c, 0:1, :] = new
            acc_ref[...] = acc_ref[...] * jnp.exp2(old - new) + dot(vt, e)

        inv = 1.0 / acc_ref[32:33, :]
        att = (acc_ref[0:32, :] * inv).astype(BF)
        attT_ref[hs, :] = att
        gp = (gT_ref[hs, :].astype(F32) * inv).astype(BF)
        delta = -jnp.sum(gp.astype(F32) * att.astype(F32), axis=0, keepdims=True)
        d0 = delta.astype(BF).astype(F32)
        d1 = (delta - d0).astype(BF).astype(F32)
        d2 = delta - d0 - d1
        gmT_ref[...] = jnp.zeros_like(gmT_ref)
        gmT_ref[hs, :] = gp
        gm_ref[...] = gmT_ref[...].T
        gmT_ref[96:112, :] = jnp.where(i16 == 0, d0, jnp.where(i16 == 1, d1, jnp.where(i16 == 2, d2, 0.0))).astype(BF)
        acc_ref[...] = jnp.zeros_like(acc_ref)

        @pl.loop(0, nk)
        def _(c):
            r = rows(c)
            ga = dot(kv_ref[r, 128:256], gmT_ref[...]).astype(BF)
            es = e_ref[r, :] * jnp.exp2(mb_ref[c, 0:1, :] - m_ref[0:1, :]).astype(BF)
            ds = es * ga
            dv = dot(es, gm_ref[...])
            dk = dot(ds, qm_ref[...]) * SCALE
            acc_ref[0:32, :] += dot(kT_ref[hs, r], ds)
            if h == 0:
                dkv_acc[r, 0:128] = dk
                dkv_acc[r, 128:256] = dv
            elif h == 1:
                dkv_acc[r, 0:128] += dk
                dkv_acc[r, 128:256] += dv
            else:
                dkv_ref[r, 0:128] = (dkv_acc[r, 0:128] + dk).astype(BF)
                dkv_ref[r, 128:256] = (dkv_acc[r, 128:256] + dv).astype(BF)

        dqT_ref[hs, :] = (acc_ref[0:32, :] * SCALE).astype(BF)

    qa_ref[:, 0:128] = dqT_ref[...].T
    qa_ref[:, 128:256] = attT_ref[...].T


def back_kernel(dkv_ref, qa_ref, cells_ref, grad_ref, wq_ref, wk_ref, wv_ref, wo_ref,
                gc_ref, gwq_ref, gwk_ref, gwv_ref, gwo_ref,
                tw, part, hp, hn, fp, fn, fin, rkv, rqa, wp, rs, p2, wf,
                qs, qr, ts, tr, hs_, hr, fs, fr, ks, kr, as_, ar, bs, br, cs, cr):
    z, x, yl, yh, c = place()
    mine = x // 2 == c
    own = jnp.where(mine, 1, 0)
    zp, zn = (z + 1) % 4, (z + 3) % 4
    zo = (z + 2) % 4
    up, down, twin = device(zp, x, yl, yh, c), device(zn, x, yl, yh, c), device(z, x, yl, yh, 1 - c)
    slot = (x % 2) * 2 + yl
    i16 = z * 4 + x
    i8 = (yh * 2 + yl) * 2 + c

    def dev16(j):
        return device(j // 4, j % 4, yl, yh, c)

    def dev8(j):
        return device(z, x, (j // 2) % 2, j // 4, j % 2)

    barrier = pltpu.get_barrier_semaphore()

    def greet(to):
        pl.semaphore_signal(barrier, inc=1, device_id=to, device_id_type=MESH)

    for to in (up, down, twin):
        greet(to)
    for j in range(4):
        @pl.when(jnp.logical_not(jnp.logical_and(mine, slot == j)))
        def _():
            greet(device(z, 2 * c + j // 2, j % 2, yh, x // 2))

    @pl.loop(1, 16)
    def _(n):
        greet(dev16((i16 + n) % 16))

    @pl.loop(1, 8)
    def _(n):
        greet(dev8((i8 + n) % 8))

    pl.semaphore_wait(barrier, 3 + 4 - own + 15 + 7)

    def back(s, src, dst, send, recv):
        q = pl.ds(s * 192, 192)
        to = device(z, 2 * c + s // 2, s % 2, yh, x // 2)
        return rcopy(src.at[q, :], dst.at[slot], send.at[s], recv.at[slot], to)

    def go_back(src, dst, send, recv):
        for s in range(4):
            keep = jnp.logical_and(mine, slot == s)

            @pl.when(keep)
            def _():
                pltpu.make_async_copy(src.at[pl.ds(s * 192, 192), :], dst.at[slot], recv.at[slot]).start()

            @pl.when(jnp.logical_not(keep))
            def _():
                back(s, src, dst, send, recv).start()

    def sent_back(src, dst, send, recv):
        for s in range(4):
            @pl.when(jnp.logical_not(jnp.logical_and(mine, slot == s)))
            def _():
                back(s, src, dst, send, recv).wait_send()

    def came_back(dst, recv):
        for j in range(4):
            pltpu.make_async_copy(dst.at[j], dst.at[j], recv.at[j]).wait()

    def block(zz, cc):
        return pl.ds(pl.multiple_of(zz * 1536 + cc * 768, 768), 768)

    sent = []

    def go(copy):
        copy.start()
        sent.append(copy)

    for n, zz in enumerate((zo, zp, zn, z)):
        go(rcopy(dkv_ref.at[block(zz, 1 - c), :], tw.at[n], ts.at[n], tr.at[n], twin))
    go_back(qa_ref, rqa, qs, qr)

    def with_twin(n, zz):
        pltpu.make_async_copy(tw.at[n], tw.at[n], tr.at[n]).wait()
        return dkv_ref[block(zz, c), :].astype(F32) + tw[n].astype(F32)

    lo, hi = pl.ds(0, 384), pl.ds(384, 384)
    part[0] = with_twin(0, zo).astype(BF)
    go(rcopy(part.at[0, lo, :], hp, hs_.at[0], hr.at[0], up))
    go(rcopy(part.at[0, hi, :], hn, hs_.at[1], hr.at[1], down))
    part[1] = with_twin(1, zp).astype(BF)
    go(rcopy(part.at[1, hi, :], fp.at[hi, :], fs.at[0], fr.at[0], up))
    part[2] = with_twin(2, zn).astype(BF)
    go(rcopy(part.at[2, lo, :], fn.at[lo, :], fs.at[1], fr.at[1], down))
    pltpu.make_async_copy(hp, hp, hr.at[0]).wait()
    part[1, 0:384, :] = (part[1, 0:384, :].astype(F32) + hp[...].astype(F32)).astype(BF)
    go(rcopy(part.at[1, lo, :], fp.at[lo, :], fs.at[2], fr.at[2], up))
    pltpu.make_async_copy(hn, hn, hr.at[1]).wait()
    part[2, 384:768, :] = (part[2, 384:768, :].astype(F32) + hn[...].astype(F32)).astype(BF)
    go(rcopy(part.at[2, hi, :], fn.at[hi, :], fs.at[3], fr.at[3], down))

    came_back(rqa, qr)
    i, j = iotas((128, E))

    def join(ref, f, a):
        left = (j == i) & (i < HALF)
        right = (j == i + HALF) & (i < HALF)
        return (
            dot(ref[2 * f, :, a], left.astype(F32).astype(BF)) + dot(ref[2 * f + 1, :, a], right.astype(F32).astype(BF))
        ).astype(BF)

    left_half, right_half = slice(0, 128), slice(128, 256)
    picks = [pick_rows(f) for f in range(2)]
    cf = [dot(p, cells_ref[...]).astype(BF) for p in picks]
    gf = [dot(p, grad_ref[...]).astype(BF) for p in picks]
    dq = [join(rqa, f, left_half) for f in range(2)]
    at = [join(rqa, f, right_half) for f in range(2)]
    wp[0:192, :] = (t_dot(cf[0], dq[0]) + t_dot(cf[1], dq[1])).astype(BF)
    wp[576:768, :] = (t_dot(at[0], gf[0]) + t_dot(at[1], gf[1])).astype(BF)
    total = [gf[f].astype(F32) + dot_t(dq[f], wq_ref[...]) for f in range(2)]

    mine_sum = with_twin(3, z)
    pltpu.make_async_copy(fp.at[hi, :], fp.at[hi, :], fr.at[0]).wait()
    pltpu.make_async_copy(fn.at[lo, :], fn.at[lo, :], fr.at[1]).wait()
    pltpu.make_async_copy(fp.at[lo, :], fp.at[lo, :], fr.at[2]).wait()
    pltpu.make_async_copy(fn.at[hi, :], fn.at[hi, :], fr.at[3]).wait()
    fin[...] = (mine_sum + fp[...].astype(F32) + fn[...].astype(F32)).astype(BF)
    go_back(fin, rkv, ks, kr)
    came_back(rkv, kr)
    dk = [join(rkv, f, left_half) for f in range(2)]
    dv = [join(rkv, f, right_half) for f in range(2)]
    wp[192:384, :] = (t_dot(cf[0], dk[0]) + t_dot(cf[1], dk[1])).astype(BF)
    wp[384:576, :] = (t_dot(cf[0], dv[0]) + t_dot(cf[1], dv[1])).astype(BF)

    def slab(n):
        return pl.ds(pl.multiple_of(n * 48, 16), 48)

    def one(n):
        to = (i16 + n) % 16
        return rcopy(wp.at[slab(to), :], rs.at[i16], as_.at[n], ar.at[i16], dev16(to))

    def two(n):
        to = (i8 + n) % 8
        return rcopy(p2.at[i8], p2.at[i8], bs.at[n], br.at[i8], dev8(to))

    def three(n):
        to = (i16 + n) % 16
        return rcopy(wf.at[slab(i16), :], wf.at[slab(i16), :], cs.at[n], cr.at[i16], dev16(to))

    @pl.loop(1, 16)
    def _(n):
        one(n).start()

    for f in range(2):
        total[f] = total[f] + dot_t(dk[f], wk_ref[...]) + dot_t(dv[f], wv_ref[...])
    gc_ref[...] = (t_dot(picks[0], total[0].astype(BF)) + t_dot(picks[1], total[1].astype(BF))).astype(BF)

    rs[i16] = wp[slab(i16), :]

    @pl.loop(1, 16)
    def _(n):
        m = (i16 + n) % 16
        pltpu.make_async_copy(rs.at[m], rs.at[m], ar.at[m]).wait()

    acc = rs[0].astype(F32)
    for n in range(1, 16):
        acc = acc + rs[n].astype(F32)
    p2[i8] = acc.astype(BF)

    @pl.loop(1, 8)
    def _(n):
        two(n).start()

    @pl.loop(1, 8)
    def _(n):
        m = (i8 + n) % 8
        pltpu.make_async_copy(p2.at[m], p2.at[m], br.at[m]).wait()

    acc = p2[0].astype(F32)
    for n in range(1, 8):
        acc = acc + p2[n].astype(F32)
    wf[slab(i16), :] = acc.astype(BF)

    @pl.loop(1, 16)
    def _(n):
        three(n).start()

    @pl.loop(1, 16)
    def _(n):
        m = (i16 + n) % 16
        pltpu.make_async_copy(wf.at[slab(m), :], wf.at[slab(m), :], cr.at[m]).wait()

    gwq_ref[...] = wf[0:192, :].astype(F32)
    gwk_ref[...] = wf[192:384, :].astype(F32)
    gwv_ref[...] = wf[384:576, :].astype(F32)
    gwo_ref[...] = wf[576:768, :].astype(F32)

    for copy in sent:
        copy.wait_send()
    sent_back(qa_ref, rqa, qs, qr)
    sent_back(fin, rkv, ks, kr)

    @pl.loop(1, 16)
    def _(n):
        one(n).wait_send()
        three(n).wait_send()

    @pl.loop(1, 8)
    def _(n):
        two(n).wait_send()


def sds(shape, dtype=BF):
    return jax.ShapeDtypeStruct(shape, dtype)


VM = pl.BlockSpec(memory_space=pltpu.VMEM)
DMA = pltpu.SemaphoreType.DMA


def share(*args):
    return pl.pallas_call(
        share_kernel,
        out_shape=[sds((NR, 256)), sds((NQ, 256))],
        in_specs=[VM] * 7,
        out_specs=[VM] * 2,
        scratch_shapes=[
            pltpu.VMEM((4, ROWS, 256), BF), pltpu.VMEM((4, ROWS, 256), BF),
            DMA((4,)), DMA((4,)), DMA((4,)), DMA((4,)), DMA((8,)), DMA((8,)), DMA((4,)), DMA((4,)), DMA((16,)), DMA((16,)),
        ],
        compiler_params=pltpu.CompilerParams(collective_id=1, has_side_effects=True, vmem_limit_bytes=40 * 2**20),
        name="share",
    )(*args)


def attention(*args):
    return pl.pallas_call(
        attention_kernel,
        out_shape=[sds((NR, 256)), sds((NQ, 256))],
        in_specs=[VM] * 2,
        out_specs=[VM] * 2,
        scratch_shapes=[
            pltpu.VMEM((NR, NQ), BF), pltpu.VMEM((NR // KC, 8, NQ), F32),
            pltpu.VMEM((128, NR), BF), pltpu.VMEM((128, NR), BF),
            pltpu.VMEM((128, NQ), BF), pltpu.VMEM((128, NQ), BF),
            pltpu.VMEM((NQ, 128), BF), pltpu.VMEM((NQ, 128), BF),
            pltpu.VMEM((128, NQ), BF), pltpu.VMEM((128, NQ), BF),
            pltpu.VMEM((48, NQ), F32), pltpu.VMEM((8, NQ), F32),
            pltpu.VMEM((NR, 256), F32),
            pltpu.VMEM((128, NQ), BF), pltpu.VMEM((128, NQ), BF),
        ],
        compiler_params=pltpu.CompilerParams(vmem_limit_bytes=56 * 2**20),
        name="attention",
    )(*args)


def finish(*args):
    w = sds((E, E), F32)
    return pl.pallas_call(
        back_kernel,
        out_shape=[sds((2 * ROWS, E)), w, w, w, w],
        in_specs=[VM] * 8,
        out_specs=[VM] * 5,
        scratch_shapes=[
            pltpu.VMEM((4, NQ, 256), BF), pltpu.VMEM((3, NQ, 256), BF),
            pltpu.VMEM((384, 256), BF), pltpu.VMEM((384, 256), BF),
            pltpu.VMEM((NQ, 256), BF), pltpu.VMEM((NQ, 256), BF), pltpu.VMEM((NQ, 256), BF),
            pltpu.VMEM((4, ROWS, 256), BF), pltpu.VMEM((4, ROWS, 256), BF),
            pltpu.VMEM((768, E), BF), pltpu.VMEM((16, 48, E), BF), pltpu.VMEM((8, 48, E), BF), pltpu.VMEM((768, E), BF),
            DMA((4,)), DMA((4,)), DMA((4,)), DMA((4,)), DMA((2,)), DMA((2,)), DMA((4,)), DMA((4,)), DMA((4,)), DMA((4,)),
            DMA((16,)), DMA((16,)), DMA((8,)), DMA((8,)), DMA((16,)), DMA((16,)),
        ],
        compiler_params=pltpu.CompilerParams(collective_id=2, has_side_effects=True, vmem_limit_bytes=40 * 2**20),
        name="finish",
    )(*args)


def body(cells, w_query, w_key, w_value, w_out, train_flag, grad_out):
    flat_cells = cells.reshape(2 * ROWS, E)
    flat_grad = grad_out.reshape(2 * ROWS, E)
    weights = (w_query, w_key, w_value, w_out)
    kv, qg = share(flat_cells, flat_grad, *weights, train_flag.reshape(ROWS, 1))
    dkv, qa = attention(kv, qg)
    grad_cells, gq, gk, gv, go = finish(dkv, qa, flat_cells, flat_grad, *weights)
    return grad_cells.reshape(cells.shape), gq, gk, gv, go


def solution(mesh):
    return jax.shard_map(
        body,
        mesh=mesh,
        in_specs=(P("row", "feat", None), P(), P(), P(), P(), P("row"), P("row", "feat", None)),
        out_specs=(P("row", "feat", None), P(), P(), P(), P()),
        check_vma=False,
    )
```

time: 1120 us -> 153 us (0.14)
  the two profiles are of different devices: /device:TPU:25 before, /device:TPU:1 now
where the time goes in v1:
time: 153 us; the launch traced here: 152 us
  Pallas kernels  136 us (89%)
  local copies, waits for them, and re-layouts  15.4 us (10%)
    pallas_call x1, Pallas kernels, attention(): pl.pallas_call(attention_kernel, out_shape=[sds((NR, 256)), sds((NQ, 256)...  56.2 us
    pallas_call x1, Pallas kernels, finish(): pl.pallas_call(back_kernel, out_shape=[sds((2 * ROWS, E)), w, w, w, w], i...  51.6 us
    pallas_call x1, Pallas kernels, share(): pl.pallas_call(share_kernel, out_shape=[sds((NR, 256)), sds((NQ, 256))],...  28.2 us
    unnamed x28, local copies, waits for them, and re-layouts  11.6 us

profile of v1, /device:TPU:1, one launch (start us, length us, event | category | flops | bytes accessed | tf_op | source)
XLA Modules:
  0.0 152.2 jit_solution(15924599016109725014)
XLA Ops:
  0.6 0.0 copy-start.11
  0.6 0.0 copy-start.9
  0.7 0.0 copy-start.7
  0.7 0.0 copy-start.5
  0.7 0.9 copy.12.flag_ref
  1.5 1.1 reshape.22.cells_ref
  2.7 1.1 reshape.23.grad_ref
  3.8 0.0 copy-start.4
  3.8 0.9 copy-done.4
  4.7 0.9 copy-done.6
  5.6 0.9 copy-done.8
  6.5 0.9 copy-done.10
  7.4 28.2 %share.1 = (bf16[6144,256]{1,0:T(8,128)(2,1)S(1)}, bf16[768,256]{1,0:T(8,128)(2,1)S(1)}) custom-call(bf16[384,192]{1,0:T(8,128)(2,1)S(1)} %reshape.22.cells_ref, bf16[384,192]{1,0:T(8,128)(2,1)S(1)} %reshape.23.grad_ref, bf16[192,192]{1,0:T(8,128)(2,1)S(1)} %copy-done.4, bf16[192,192]{1,0:T(8,128)(2,1)S(1)} %copy-done.6, bf16[192,192]{1,0:T(8,128)(2,1)S(1)} %copy-done.8, ...), custom_call_target="tpu_custom_call" | custom-call | tf_op jit(solution)/shard_map/share/pallas_call | solution.py:500
  35.6 1.6 %copy-done = bf16[6144,256]{1,0:T(8,128)(2,1)} copy-done((bf16[6144,256]{1,0:T(8,128)(2,1)}, bf16[6144,256]{1,0:T(8,128)(2,1)S(1)}, u32[]{:S(2)}) %copy-start) | copy-done | bytes 3145752
  37.2 0.8 copy-done.3
  38.0 56.2 %attention.1 = (bf16[6144,256]{1,0:T(8,128)(2,1)}, bf16[768,256]{1,0:T(8,128)(2,1)}) custom-call(bf16[6144,256]{1,0:T(8,128)(2,1)} %copy-done, bf16[768,256]{1,0:T(8,128)(2,1)} %copy-done.3), custom_call_target="tpu_custom_call" | custom-call | tf_op jit(solution)/shard_map/attention/pallas_call | solution.py:515
  94.2 1.9 %copy-done.1 = bf16[6144,256]{1,0:T(8,128)(2,1)S(1)} copy-done((bf16[6144,256]{1,0:T(8,128)(2,1)S(1)}, bf16[6144,256]{1,0:T(8,128)(2,1)}, u32[]{:S(2)}) %copy-start.1) | copy-done | bytes 3145752
  96.1 1.0 copy-done.2
  97.1 51.6 %finish.1 = (bf16[384,192]{1,0:T(8,128)(2,1)S(1)}, f32[192,192]{1,0:T(8,128)S(1)}, f32[192,192]{1,0:T(8,128)S(1)}, f32[192,192]{1,0:T(8,128)S(1)}, f32[192,192]{1,0:T(8,128)S(1)}) custom-call(bf16[6144,256]{1,0:T(8,128)(2,1)S(1)} %copy-done.1, bf16[768,256]{1,0:T(8,128)(2,1)S(1)} %copy-done.2, bf16[384,192]{1,0:T(8,128)(2,1)S(1)} %reshape.22.cells_ref, ...), custom_call_target="tpu_custom_call" | custom-call | tf_op jit(solution)/shard_map/finish/pallas_call | solution.py:537
  148.7 0.8 reshape.25
  149.5 0.7 copy.17
  150.2 0.7 copy.18
  150.9 0.7 copy.19
  151.5 0.7 copy.20
  (11 shorter events, 0.0 us)
Async XLA Ops:
  0.6 93.6 %copy-start.11 = (bf16[192,192]{1,0:T(8,128)(2,1)S(1)}, bf16[192,192]{1,0:T(8,128)(2,1)}, u32[]{:S(2)}) copy-start(bf16[192,192]{1,0:T(8,128)(2,1)} %wo_ref.3) | copy-start | bytes 221188
  0.6 93.6 %copy-start.9 = (bf16[192,192]{1,0:T(8,128)(2,1)S(1)}, bf16[192,192]{1,0:T(8,128)(2,1)}, u32[]{:S(2)}) copy-start(bf16[192,192]{1,0:T(8,128)(2,1)} %wv_ref.3) | copy-start | bytes 221188
  0.7 93.5 %copy-start.7 = (bf16[192,192]{1,0:T(8,128)(2,1)S(1)}, bf16[192,192]{1,0:T(8,128)(2,1)}, u32[]{:S(2)}) copy-start(bf16[192,192]{1,0:T(8,128)(2,1)} %wk_ref.3) | copy-start | bytes 221188
  0.7 93.5 %copy-start.5 = (bf16[192,192]{1,0:T(8,128)(2,1)S(1)}, bf16[192,192]{1,0:T(8,128)(2,1)}, u32[]{:S(2)}) copy-start(bf16[192,192]{1,0:T(8,128)(2,1)} %wq_ref.3) | copy-start | bytes 221188
  3.8 0.9 copy-start.4
  4.7 0.9 copy-start.6
  5.6 0.9 copy-start.8
  6.5 0.9 copy-start.10
  35.6 1.6 %copy-start = (bf16[6144,256]{1,0:T(8,128)(2,1)}, bf16[6144,256]{1,0:T(8,128)(2,1)S(1)}, u32[]{:S(2)}) copy-start(bf16[6144,256]{1,0:T(8,128)(2,1)S(1)} %get-tuple-element.14.kv_ref) | copy-start | bytes 9437188
  37.2 0.8 copy-start.3
  94.2 1.9 %copy-start.1 = (bf16[6144,256]{1,0:T(8,128)(2,1)S(1)}, bf16[6144,256]{1,0:T(8,128)(2,1)}, u32[]{:S(2)}) copy-start(bf16[6144,256]{1,0:T(8,128)(2,1)} %get-tuple-element.16.dkv_ref) | copy-start | bytes 9437188
  96.1 1.0 copy-start.2

commit v2 on v1

v2 whole, which is shorter than its diff:
```python
import jax
import jax.numpy as jnp
from jax import lax
from jax.experimental import pallas as pl
from jax.experimental.pallas import tpu as pltpu
from jax.sharding import PartitionSpec as P


HD = 32
SCALE = float(HD) ** -0.5
SCALE_LOG2E = SCALE * 1.4426950408889634
BIAS = -1e30
F32 = jnp.float32
BF = jnp.bfloat16
MESH = pl.DeviceIdType.MESH

E = 192
HALF = 96
ROWS = 192
NQ = 768
NR = 6144
KC = 768
PC = 384
BLOCKS = 8


def dot(a, b):
    return jnp.dot(a, b, preferred_element_type=F32)


def t_dot(a, b):
    return lax.dot_general(a, b, (((0,), (0,)), ((), ())), preferred_element_type=F32)


def place():
    row = lax.axis_index("row")
    feat = lax.axis_index("feat")
    return row // 8, (row // 2) % 4, row % 2, feat // 2, feat % 2


def device(z, x, yl, yh, c):
    return ((z * 4 + x) * 2 + yl, yh * 2 + c)


def iotas(shape):
    return lax.broadcasted_iota(jnp.int32, shape, 0), lax.broadcasted_iota(jnp.int32, shape, 1)


def ones_where(mask):
    return mask.astype(F32).astype(BF)


def shifted(shape, by, most=None):
    i, j = iotas(shape)
    mask = j == i + by
    if most is not None:
        mask = mask & (i < most)
    return ones_where(mask)


def by_feature():
    i, j = iotas((2 * ROWS, 2 * ROWS))
    second = i >= ROWS
    return ones_where(j == jnp.where(second, 2 * (i - ROWS) + 1, 2 * i))


def rcopy(src, dst, send, recv, to):
    return pltpu.make_async_remote_copy(
        src_ref=src, dst_ref=dst, send_sem=send, recv_sem=recv, device_id=to, device_id_type=MESH
    )


def wait_for(ref, sem):
    pltpu.make_async_copy(ref, ref, sem).wait()


def share_kernel(cells_ref, grad_ref, flag_ref, pk_ref, gp_ref, cnt_ref,
                 cs, gs, cb, zb, s1, r1, s2, r2, zs, zr, fs, fr, ts, tr, ns, nr, ms, mr):
    z, x, yl, yh, c = place()
    mine = x // 2 == c
    own = jnp.where(mine, 1, 0)
    zp, zo, zn = (z + 1) % 4, (z + 2) % 4, (z + 3) % 4
    up, down, twin = device(zp, x, yl, yh, c), device(zn, x, yl, yh, c), device(z, x, yl, yh, 1 - c)
    slot = (x % 2) * 2 + yl
    i8 = x * 2 + yl

    def dev8(n):
        return device(z, n // 2, n % 2, yh, c)

    barrier = pltpu.get_barrier_semaphore()

    def greet(to):
        pl.semaphore_signal(barrier, inc=1, device_id=to, device_id_type=MESH)

    for s in range(4):
        @pl.when(jnp.logical_not(jnp.logical_and(mine, slot == s)))
        def _():
            greet(device(z, 2 * c + s // 2, s % 2, yh, x // 2))
    for to in (up, down, twin):
        greet(to)
    for n in range(1, 8):
        greet(dev8((i8 + n) % 8))
    for n in range(1, 4):
        greet(device((z + n) % 4, x, yl, yh, c))

    sort = by_feature()
    left, right = shifted((ROWS, 2 * E), 0), shifted((ROWS, 2 * E), E)

    def pack(ref, out):
        rows = dot(sort, ref[...].reshape(2 * ROWS, E)).astype(BF)
        for f in range(2):
            r = f * ROWS
            out[f] = (dot(rows[r:r + HALF], left) + dot(rows[r + HALF:r + ROWS], right)).astype(BF)

    pack(cells_ref, cs)
    pack(grad_ref, gs)

    def add(n, total):
        return total + flag_ref[n]

    flags = lax.fori_loop(0, ROWS, add, jnp.int32(0), unroll=16)
    cb[i8] = jnp.full((8, 128), flags.astype(F32), F32)

    pl.semaphore_wait(barrier, 4 - own + 3 + 7 + 3)

    my_rows = pl.ds(pl.multiple_of(((z * 4 + x) * 2 + yl) * HALF, HALF), HALF)
    my_slot = pl.ds(pl.multiple_of(slot * HALF, HALF), HALF)

    def first(j):
        to = device(z, 2 * c + j // 2, j % 2, yh, x // 2)
        a = rcopy(cs.at[j // 2], pk_ref.at[my_rows, :], s1.at[j], r1.at[slot], to)
        b = rcopy(gs.at[j // 2], gp_ref.at[my_slot, :], s2.at[j], r2.at[slot], to)
        return a, b

    for j in range(4):
        keep = jnp.logical_and(mine, slot == j)

        @pl.when(keep)
        def _():
            pltpu.make_async_copy(cs.at[j // 2], pk_ref.at[my_rows, :], r1.at[slot]).start()

        @pl.when(jnp.logical_not(keep))
        def _():
            first(j)[0].start()

    def plane(n):
        return rcopy(cb.at[i8], cb.at[i8], ns.at[n], nr.at[i8], dev8((i8 + n) % 8))

    def column(n):
        return rcopy(zb.at[z], zb.at[z], ms.at[n], mr.at[z], device((z + n) % 4, x, yl, yh, c))

    def rows_of(zz, cc, s):
        return pl.ds(pl.multiple_of((zz * 2 + cc) * PC + s * HALF, HALF), HALF)

    def move(zz, s, send, recv, to):
        r = rows_of(zz, c, s)
        return rcopy(pk_ref.at[r, :], pk_ref.at[r, :], send, recv, to)

    def landed(zz, cc, s, recv):
        wait_for(pk_ref.at[rows_of(zz, cc, s), :], recv)

    sent = []

    def go(copy):
        copy.start()
        sent.append(copy)

    for s in range(4):
        landed(z, c, s, r1.at[s])
        go(move(z, s, zs.at[s], zr.at[s], up))
        go(move(z, s, zs.at[4 + s], zr.at[4 + s], down))
        go(move(z, s, ts.at[s], tr.at[s], twin))

    for n in range(1, 8):
        go(plane(n))
    for j in range(4):
        keep = jnp.logical_and(mine, slot == j)

        @pl.when(keep)
        def _():
            pltpu.make_async_copy(gs.at[j // 2], gp_ref.at[my_slot, :], r2.at[slot]).start()

        @pl.when(jnp.logical_not(keep))
        def _():
            first(j)[1].start()

    for i in range(4):
        s = i
        landed(zn, c, s, zr.at[s])
        if s < 2:
            go(move(zn, s, fs.at[s], fr.at[s], up))
        go(move(zn, s, ts.at[4 + s], tr.at[4 + s], twin))
        s = (i + 2) % 4
        landed(zp, c, s, zr.at[4 + s])
        if s >= 2:
            go(move(zp, s, fs.at[s], fr.at[s], down))
        go(move(zp, s, ts.at[8 + s], tr.at[8 + s], twin))

    for n in range(1, 8):
        m = (i8 + n) % 8
        wait_for(cb.at[m], nr.at[m])
    total = cb[0]
    for n in range(1, 8):
        total = total + cb[n]
    zb[z] = total
    for n in range(1, 4):
        go(column(n))

    for s in (0, 2, 1, 3):
        landed(zo, c, s, fr.at[s])
        go(move(zo, s, ts.at[12 + s], tr.at[12 + s], twin))

    for n in range(1, 4):
        m = (z + n) % 4
        wait_for(zb.at[m], mr.at[m])
    cnt_ref[...] = zb[0] + zb[1] + zb[2] + zb[3]

    for n, zz in ((0, z), (1, zn), (2, zp), (3, zo)):
        for s in range(4):
            landed(zz, 1 - c, s, tr.at[4 * n + s])
    for s in range(4):
        wait_for(gp_ref.at[pl.ds(s * HALF, HALF), :], r2.at[s])
    for copy in sent:
        copy.wait_send()
    for j in range(4):
        @pl.when(jnp.logical_not(jnp.logical_and(mine, slot == j)))
        def _():
            a, b = first(j)
            a.wait_send()
            b.wait_send()


def attention_kernel(pk_ref, gp_ref, cnt_ref, wq_ref, wk_ref, wv_ref, wo_ref, g_ref, gq_ref, w_ref,
                     e_ref, mb_ref, kv_ref, kT_ref, vT_ref, pT_ref, qT_ref, gT_ref, qm_ref, gm_ref,
                     qmT_ref, gmT_ref, acc_ref, m_ref, dkv_acc, dkv_ref, attT_ref, dqT_ref, wacc_ref,
                     wkva, wkvb, wqa, wqb, wga, wgb, ua, ub):
    z, x, yl, yh, c = place()
    train = jnp.max(cnt_ref[...]).astype(jnp.int32)
    nk = lax.div(train + KC - 1, KC)

    def rows(n):
        return pl.ds(pl.multiple_of(n * KC, KC), KC)

    def packs(n):
        return pl.ds(pl.multiple_of(n * PC, PC), PC)

    @pl.loop(nk, BLOCKS)
    def _(n):
        g_ref[packs(n), :] = jnp.zeros((PC, 384), BF)

    i, j = iotas((E, 128))
    heads = ones_where((i == j + HALF * yl) & (j < HALF))
    wq = dot(wq_ref[...], heads).astype(BF)
    wk = dot(wk_ref[...], heads).astype(BF)
    wv = dot(wv_ref[...], heads).astype(BF)
    wo = t_dot(wo_ref[...], heads).astype(BF)
    for a, b, w in ((wkva, wkvb, jnp.concatenate([wk, wv], 1)), (wqa, wqb, wq), (wga, wgb, wo)):
        a[0:192, :] = w
        a[192:256, :] = jnp.zeros((64, w.shape[1]), BF)
        b[64:256, :] = w
        b[0:64, :] = jnp.zeros((64, w.shape[1]), BF)
    left, right = shifted((E, 2 * E), 0), shifted((E, 2 * E), E)
    for n, w in enumerate((wk, wv, wq)):
        ua[128 * n:128 * n + 128, :] = t_dot(w, left).astype(BF)
        ub[128 * n:128 * n + 128, :] = t_dot(w, right).astype(BF)

    lane = lax.broadcasted_iota(jnp.int32, (PC, 128), 1)
    sub = lax.broadcasted_iota(jnp.int32, (PC, 128), 0)
    real = sub + 96 * ((sub >= 96).astype(jnp.int32) + (sub >= 192).astype(jnp.int32) + (sub >= 288).astype(jnp.int32))
    v_extra = jnp.where((lane >= HALF) & (lane < HALF + 3), 1.0, 0.0)

    @pl.loop(0, nk)
    def _(n):
        p = pk_ref[packs(n), :]
        pT_ref[:, packs(n)] = p.T
        for h, (part, w) in enumerate(((p[:, 0:256], wkva), (p[:, 128:384], wkvb))):
            kv = dot(part, w[...])
            bias = jnp.where((lane == HALF) & (real + (n * KC + HALF * h) >= train), BIAS, 0.0)
            r = pl.ds(pl.multiple_of(n * KC + PC * h, PC), PC)
            k = (kv[:, 0:128] + bias).astype(BF)
            v = (kv[:, 128:256] + v_extra).astype(BF)
            kv_ref[r, 0:128] = k
            kv_ref[r, 128:256] = v
            kT_ref[:, r] = k.T
            vT_ref[:, r] = v.T

    block = z * 2 + c
    po = pk_ref[packs(block), :]
    go = gp_ref[...]
    for src, a, b, out in ((po, wqa, wqb, qT_ref), (go, wga, wgb, gT_ref)):
        out[:, 0:PC] = dot(src[:, 0:256], a[...]).astype(BF).T
        out[:, PC:NQ] = dot(src[:, 128:384], b[...]).astype(BF).T
    attT_ref[...] = jnp.zeros_like(attT_ref)
    dqT_ref[...] = jnp.zeros_like(dqT_ref)
    wacc_ref[...] = jnp.zeros_like(wacc_ref)
    i16 = lax.broadcasted_iota(jnp.int32, (16, NQ), 0)

    for h in range(3):
        hs = slice(32 * h, 32 * h + 32)
        qmT_ref[...] = jnp.zeros_like(qmT_ref)
        qmT_ref[hs, :] = qT_ref[hs, :]
        qm_ref[...] = qmT_ref[...].T
        qmT_ref[96:112, :] = jnp.where(i16 == 0, 1.0, 0.0).astype(BF)
        acc_ref[...] = jnp.zeros_like(acc_ref)
        m_ref[...] = jnp.full_like(m_ref, BIAS)

        @pl.loop(0, nk)
        def _(n):
            r = rows(n)
            vt = jnp.concatenate([vT_ref[hs, r], vT_ref[96:112, r]], 0)
            s = dot(kv_ref[r, 0:128], qmT_ref[...]) * SCALE_LOG2E
            old = m_ref[0:1, :]
            new = jnp.maximum(old, jnp.ceil(jnp.max(s, axis=0, keepdims=True)))
            e = jnp.exp2(s - new).astype(BF)
            e_ref[r, :] = e
            m_ref[0:1, :] = new
            mb_ref[n, 0:1, :] = new
            acc_ref[...] = acc_ref[...] * jnp.exp2(old - new) + dot(vt, e)

        inv = 1.0 / acc_ref[32:33, :]
        att = (acc_ref[0:32, :] * inv).astype(BF)
        attT_ref[hs, :] = att
        gp = (gT_ref[hs, :].astype(F32) * inv).astype(BF)
        delta = -jnp.sum(gp.astype(F32) * att.astype(F32), axis=0, keepdims=True)
        d0 = delta.astype(BF).astype(F32)
        d1 = (delta - d0).astype(BF).astype(F32)
        d2 = delta - d0 - d1
        gmT_ref[...] = jnp.zeros_like(gmT_ref)
        gmT_ref[hs, :] = gp
        gm_ref[...] = gmT_ref[...].T
        gmT_ref[96:112, :] = jnp.where(i16 == 0, d0, jnp.where(i16 == 1, d1, jnp.where(i16 == 2, d2, 0.0))).astype(BF)
        acc_ref[...] = jnp.zeros_like(acc_ref)

        @pl.loop(0, nk)
        def _(n):
            r = rows(n)
            ga = dot(kv_ref[r, 128:256], gmT_ref[...]).astype(BF)
            es = e_ref[r, :] * jnp.exp2(mb_ref[n, 0:1, :] - m_ref[0:1, :]).astype(BF)
            ds = es * ga
            dv = dot(es, gm_ref[...])
            dk = dot(ds, qm_ref[...]) * SCALE
            acc_ref[0:32, :] += dot(kT_ref[hs, r], ds)
            if h == 0:
                dkv_acc[r, 0:128] = dk
                dkv_acc[r, 128:256] = dv
            elif h == 1:
                dkv_acc[r, 0:128] += dk
                dkv_acc[r, 128:256] += dv
            else:
                dkv_ref[:, 0:128] = (dkv_acc[r, 0:128] + dk).astype(BF)
                dkv_ref[:, 128:256] = (dkv_acc[r, 128:256] + dv).astype(BF)
                da, db = dkv_ref[0:PC, :], dkv_ref[PC:KC, :]
                g_ref[packs(n), :] = (dot(da, ua[0:256, :]) + dot(db, ub[0:256, :])).astype(BF)
                wacc_ref[...] += dot(pT_ref[0:E, packs(n)], da) + dot(pT_ref[E:2 * E, packs(n)], db)

        dqT_ref[hs, :] = (acc_ref[0:32, :] * SCALE).astype(BF)

    dq, at = dqT_ref[...].T, attT_ref[...].T
    gq_ref[...] = dot(dq[0:PC], ua[256:384, :]) + dot(dq[PC:NQ], ub[256:384, :])
    poT, goT = po.T, go.T
    w_q = dot(poT[0:E], dq[0:PC]) + dot(poT[E:2 * E], dq[PC:NQ])
    w_o = dot(goT[0:E], at[0:PC]) + dot(goT[E:2 * E], at[PC:NQ])
    w_ref[...] = (
        dot(w_q.astype(BF), shifted((128, 384), 0, HALF))
        + dot(w_o.astype(BF), shifted((128, 384), HALF, HALF))
        + dot(wacc_ref[:, 0:128].astype(BF), shifted((128, 384), 2 * HALF, HALF))
        + dot(wacc_ref[:, 128:256].astype(BF), shifted((128, 384), 3 * HALF, HALF))
    ).astype(BF)


def reduce_kernel(g_ref, gq_ref, w_ref, ret_ref, wf_ref,
                  tw, part, hp, hn, fp, fn, fin, rs, p2,
                  ts, tr, hs_, hr, fs, fr, ks, kr, as_, ar, bs, br, cs, cr):
    z, x, yl, yh, c = place()
    mine = x // 2 == c
    own = jnp.where(mine, 1, 0)
    zp, zo, zn = (z + 1) % 4, (z + 2) % 4, (z + 3) % 4
    up, down, twin = device(zp, x, yl, yh, c), device(zn, x, yl, yh, c), device(z, x, yl, yh, 1 - c)
    slot = (x % 2) * 2 + yl
    i16 = z * 4 + x
    i8 = (yh * 2 + yl) * 2 + c
    owner = i16 < SLABS
    owns = jnp.where(owner, 1, 0)

    def dev16(n):
        return device(n // 4, n % 4, yl, yh, c)

    def dev8(n):
        return device(z, x, (n // 2) % 2, n // 4, n % 2)

    barrier = pltpu.get_barrier_semaphore()

    def greet(to):
        pl.semaphore_signal(barrier, inc=1, device_id=to, device_id_type=MESH)

    for to in (twin, up, down):
        greet(to)
    for j in range(4):
        @pl.when(jnp.logical_not(jnp.logical_and(mine, slot == j)))
        def _():
            greet(device(z, 2 * c + j // 2, j % 2, yh, x // 2))

    @pl.loop(1, 16)
    def _(n):
        greet(dev16((i16 + n) % 16))

    @pl.loop(1, 8)
    def _(n):
        greet(dev8((i8 + n) % 8))

    pl.semaphore_wait(barrier, 3 + 4 - own + 15 + 7)

    sent = []

    def go(copy):
        copy.start()
        sent.append(copy)

    def block(zz, cc):
        return pl.ds(pl.multiple_of((zz * 2 + cc) * PC, PC), PC)

    for n, zz in enumerate((zo, zp, zn, z)):
        go(rcopy(g_ref.at[block(zz, 1 - c), :], tw.at[n], ts.at[n], tr.at[n], twin))

    def slab(n):
        return pl.ds(pl.multiple_of(n * 16, 16), 16)

    def one(n):
        to = (i16 + n) % 16
        return to < SLABS, rcopy(w_ref.at[slab(jnp.minimum(to, SLABS - 1)), :], rs.at[i16], as_.at[n], ar.at[i16], dev16(to))

    def two(n):
        return rcopy(p2.at[i8], p2.at[i8], bs.at[n], br.at[i8], dev8((i8 + n) % 8))

    def three(n):
        mine_ = slab(jnp.minimum(i16, SLABS - 1))
        return rcopy(wf_ref.at[:, mine_, :], wf_ref.at[:, mine_, :], cs.at[n], cr.at[i16], dev16((i16 + n) % 16))

    @pl.loop(1, 16)
    def _(n):
        ok, copy = one(n)

        @pl.when(ok)
        def _():
            copy.start()

    def with_twin(n, zz):
        wait_for(tw.at[n], tr.at[n])
        return g_ref[block(zz, c), :].astype(F32) + tw[n].astype(F32)

    lo, hi = pl.ds(0, 192), pl.ds(192, 192)
    part[0] = with_twin(0, zo).astype(BF)
    go(rcopy(part.at[0, lo, :], hp, hs_.at[0], hr.at[0], up))
    go(rcopy(part.at[0, hi, :], hn, hs_.at[1], hr.at[1], down))
    part[1] = with_twin(1, zp).astype(BF)
    go(rcopy(part.at[1, hi, :], fp.at[hi, :], fs.at[0], fr.at[0], up))
    part[2] = with_twin(2, zn).astype(BF)
    go(rcopy(part.at[2, lo, :], fn.at[lo, :], fs.at[1], fr.at[1], down))

    @pl.when(owner)
    def _():
        rs[i16] = w_ref[slab(jnp.minimum(i16, SLABS - 1)), :]

        @pl.loop(1, 16)
        def _(n):
            m = (i16 + n) % 16
            wait_for(rs.at[m], ar.at[m])

        acc = rs[0].astype(F32)
        for n in range(1, 16):
            acc = acc + rs[n].astype(F32)
        p2[i8] = acc.astype(BF)

        @pl.loop(1, 8)
        def _(n):
            two(n).start()

    wait_for(hp, hr.at[0])
    part[1, 0:192, :] = (part[1, 0:192, :].astype(F32) + hp[...].astype(F32)).astype(BF)
    go(rcopy(part.at[1, lo, :], fp.at[lo, :], fs.at[2], fr.at[2], up))
    wait_for(hn, hr.at[1])
    part[2, 192:384, :] = (part[2, 192:384, :].astype(F32) + hn[...].astype(F32)).astype(BF)
    go(rcopy(part.at[2, hi, :], fn.at[hi, :], fs.at[3], fr.at[3], down))

    @pl.when(owner)
    def _():
        @pl.loop(1, 8)
        def _(n):
            m = (i8 + n) % 8
            wait_for(p2.at[m], br.at[m])

        for half in range(2):
            n = 2 * half
            acc = p2[n].astype(F32) + p2[n + 1].astype(F32) + p2[n + 4].astype(F32) + p2[n + 5].astype(F32)
            wf_ref[half, slab(jnp.minimum(i16, SLABS - 1)), :] = acc.astype(BF)

        @pl.loop(1, 16)
        def _(n):
            three(n).start()

    total = with_twin(3, z) + gq_ref[...]
    wait_for(fp.at[hi, :], fr.at[0])
    wait_for(fn.at[lo, :], fr.at[1])
    wait_for(fp.at[lo, :], fr.at[2])
    wait_for(fn.at[hi, :], fr.at[3])
    fin[...] = (total + fp[...].astype(F32) + fn[...].astype(F32)).astype(BF)

    def back(s):
        to = device(z, 2 * c + s // 2, s % 2, yh, x // 2)
        return rcopy(fin.at[pl.ds(s * HALF, HALF), :], ret_ref.at[slot], ks.at[s], kr.at[slot], to)

    for s in range(4):
        keep = jnp.logical_and(mine, slot == s)

        @pl.when(keep)
        def _():
            pltpu.make_async_copy(fin.at[pl.ds(s * HALF, HALF), :], ret_ref.at[slot], kr.at[slot]).start()

        @pl.when(jnp.logical_not(keep))
        def _():
            back(s).start()

    for n in range(4):
        wait_for(ret_ref.at[n], kr.at[n])

    @pl.loop(1, 16)
    def _(n):
        m = (i16 + n) % 16

        @pl.when(m < SLABS)
        def _():
            r = slab(jnp.minimum(m, SLABS - 1))
            wait_for(wf_ref.at[:, r, :], cr.at[m])

    for copy in sent:
        copy.wait_send()
    for s in range(4):
        @pl.when(jnp.logical_not(jnp.logical_and(mine, slot == s)))
        def _():
            back(s).wait_send()

    @pl.loop(1, 16)
    def _(n):
        ok, copy = one(n)

        @pl.when(ok)
        def _():
            copy.wait_send()

        @pl.when(owner)
        def _():
            three(n).wait_send()

    @pl.when(owner)
    def _():
        @pl.loop(1, 8)
        def _(n):
            two(n).wait_send()


def final_kernel(ret_ref, wf_ref, grad_ref, gc_ref, gwq_ref, gwk_ref, gwv_ref, gwo_ref):
    sort = by_feature()
    i, j = iotas((256, E))
    right = ones_where(i == j + 64)
    total = grad_ref[...].reshape(2 * ROWS, E).astype(F32)
    for half in range(2):
        parts = []
        for f in range(2):
            r = ret_ref[2 * f + half]
            parts += [r[:, 0:E], dot(r[:, 128:384], right).astype(BF)]
        total = total + t_dot(sort, jnp.concatenate(parts, 0))
    gc_ref[...] = total.astype(BF).reshape(ROWS, 2, E)

    i, j = iotas((384, E))

    def weight(first):
        low = ones_where((i == j + first) & (j < HALF))
        high = ones_where((i == j - HALF + first) & (j >= HALF))
        return dot(wf_ref[0], low) + dot(wf_ref[1], high)

    gwq_ref[...] = weight(0)
    gwo_ref[...] = weight(HALF).T
    gwk_ref[...] = weight(2 * HALF)
    gwv_ref[...] = weight(3 * HALF)


SLABS = 12
VM = pl.BlockSpec(memory_space=pltpu.VMEM)
SM = pl.BlockSpec(memory_space=pltpu.SMEM)
DMA = pltpu.SemaphoreType.DMA


def sds(shape, dtype=BF):
    return jax.ShapeDtypeStruct(shape, dtype)


def share(*args):
    return pl.pallas_call(
        share_kernel,
        out_shape=[sds((NR // 2, 384)), sds((PC, 384)), sds((8, 128), F32)],
        in_specs=[VM, VM, SM],
        out_specs=[VM] * 3,
        scratch_shapes=[
            pltpu.VMEM((2, HALF, 384), BF), pltpu.VMEM((2, HALF, 384), BF),
            pltpu.VMEM((8, 8, 128), F32), pltpu.VMEM((4, 8, 128), F32),
            DMA((4,)), DMA((4,)), DMA((4,)), DMA((4,)), DMA((8,)), DMA((8,)), DMA((4,)), DMA((4,)), DMA((16,)), DMA((16,)),
            DMA((8,)), DMA((8,)), DMA((4,)), DMA((4,)),
        ],
        compiler_params=pltpu.CompilerParams(collective_id=1, has_side_effects=True, vmem_limit_bytes=24 * 2**20),
        name="share",
    )(*args)


def attention(*args):
    return pl.pallas_call(
        attention_kernel,
        out_shape=[sds((NR // 2, 384)), sds((PC, 384), F32), sds((E, 384))],
        in_specs=[VM] * 7,
        out_specs=[VM] * 3,
        scratch_shapes=[
            pltpu.VMEM((NR, NQ), BF), pltpu.VMEM((BLOCKS, 8, NQ), F32), pltpu.VMEM((NR, 256), BF),
            pltpu.VMEM((128, NR), BF), pltpu.VMEM((128, NR), BF), pltpu.VMEM((384, NR // 2), BF),
            pltpu.VMEM((128, NQ), BF), pltpu.VMEM((128, NQ), BF),
            pltpu.VMEM((NQ, 128), BF), pltpu.VMEM((NQ, 128), BF),
            pltpu.VMEM((128, NQ), BF), pltpu.VMEM((128, NQ), BF),
            pltpu.VMEM((48, NQ), F32), pltpu.VMEM((8, NQ), F32),
            pltpu.VMEM((NR, 256), F32), pltpu.VMEM((KC, 256), BF),
            pltpu.VMEM((128, NQ), BF), pltpu.VMEM((128, NQ), BF), pltpu.VMEM((E, 256), F32),
            pltpu.VMEM((256, 256), BF), pltpu.VMEM((256, 256), BF), pltpu.VMEM((256, 128), BF), pltpu.VMEM((256, 128), BF),
            pltpu.VMEM((256, 128), BF), pltpu.VMEM((256, 128), BF), pltpu.VMEM((384, 384), BF), pltpu.VMEM((384, 384), BF),
        ],
        compiler_params=pltpu.CompilerParams(vmem_limit_bytes=VLIM * 2**20),
        name="attention",
    )(*args)


VLIM = 46


def reduce(*args):
    return pl.pallas_call(
        reduce_kernel,
        out_shape=[sds((4, HALF, 384)), sds((2, E, 384))],
        in_specs=[VM] * 3,
        out_specs=[VM] * 2,
        scratch_shapes=[
            pltpu.VMEM((4, PC, 384), BF), pltpu.VMEM((3, PC, 384), BF),
            pltpu.VMEM((192, 384), BF), pltpu.VMEM((192, 384), BF),
            pltpu.VMEM((PC, 384), BF), pltpu.VMEM((PC, 384), BF), pltpu.VMEM((PC, 384), BF),
            pltpu.VMEM((16, 16, 384), BF), pltpu.VMEM((8, 16, 384), BF),
            DMA((4,)), DMA((4,)), DMA((2,)), DMA((2,)), DMA((4,)), DMA((4,)), DMA((4,)), DMA((4,)),
            DMA((16,)), DMA((16,)), DMA((8,)), DMA((8,)), DMA((16,)), DMA((16,)),
        ],
        compiler_params=pltpu.CompilerParams(collective_id=2, has_side_effects=True, vmem_limit_bytes=24 * 2**20),
        name="reduce",
    )(*args)


def final(*args):
    w = sds((E, E), F32)
    return pl.pallas_call(
        final_kernel,
        out_shape=[sds((ROWS, 2, E)), w, w, w, w],
        in_specs=[VM] * 3,
        out_specs=[VM] * 5,
        compiler_params=pltpu.CompilerParams(vmem_limit_bytes=24 * 2**20),
        name="final",
    )(*args)


def body(cells, w_query, w_key, w_value, w_out, train_flag, grad_out):
    packs, grads, count = share(cells, grad_out, train_flag)
    g, gq, w = attention(packs, grads, count, w_query, w_key, w_value, w_out)
    ret, wf = reduce(g, gq, w)
    return final(ret, wf, grad_out)


def solution(mesh):
    return jax.shard_map(
        body,
        mesh=mesh,
        in_specs=(P("row", "feat", None), P(), P(), P(), P(), P("row"), P("row", "feat", None)),
        out_specs=(P("row", "feat", None), P(), P(), P(), P()),
        check_vma=False,
    )
```

time: 153 us -> 116 us (0.76)
  the two profiles are of different devices: /device:TPU:1 before, /device:TPU:25 now
where the time goes in v2:
time: 116 us
  Pallas kernels  109 us (94%)
  local copies, waits for them, and re-layouts  6.09 us (5%)
    pallas_call x1, Pallas kernels, attention(): pl.pallas_call(attention_kernel, out_shape=[sds((NR // 2, 384)), sds((PC,...  53.4 us
    pallas_call x1, Pallas kernels, reduce(): pl.pallas_call(reduce_kernel, out_shape=[sds((4, HALF, 384)), sds((2, E,...  29.3 us
    pallas_call x1, Pallas kernels, share(): pl.pallas_call(share_kernel, out_shape=[sds((NR // 2, 384)), sds((PC, 384...  24.6 us
    unnamed x16, local copies, waits for them, and re-layouts  6.09 us

profile of v2, /device:TPU:25, one launch (start us, length us, event | category | flops | bytes accessed | tf_op | source)
XLA Modules:
  0.0 116.0 jit_solution(12698508019483184453)
XLA Ops:
  0.6 0.0 copy-start
  0.6 0.9 copy-done
  1.6 0.0 copy-start.2
  1.6 0.9 copy-done.2
  2.5 0.0 copy-start.7
  2.5 0.7 copy-done.7
  3.2 24.6 %share.1 = (bf16[3072,384]{1,0:T(8,128)(2,1)S(1)}, bf16[384,384]{1,0:T(8,128)(2,1)S(1)}, f32[8,128]{1,0:T(8,128)S(1)}) custom-call(bf16[192,2,192]{2,1,0:T(2,128)(2,1)S(1)} %copy-done.2, bf16[192,2,192]{2,1,0:T(2,128)(2,1)S(1)} %copy-done, s32[192]{0:T(256)S(1)} %copy-done.7), custom_call_target="tpu_custom_call" | custom-call | tf_op jit(solution)/shard_map/share/pallas_call | solution.py:598
  27.8 0.0 copy-start.3
  27.8 0.9 copy-done.3
  28.7 0.0 copy-start.4
  28.7 0.9 copy-done.4
  29.6 0.0 copy-start.5
  29.6 0.9 copy-done.5
  30.5 0.0 copy-start.6
  30.5 0.9 copy-done.6
  31.4 0.0 copy-start.1
  31.4 53.4 %attention.1 = (bf16[3072,384]{1,0:T(8,128)(2,1)S(1)}, f32[384,384]{1,0:T(8,128)S(1)}, bf16[192,384]{1,0:T(8,128)(2,1)S(1)}) custom-call(bf16[3072,384]{1,0:T(8,128)(2,1)S(1)} %get-tuple-element.13.pk_ref, bf16[384,384]{1,0:T(8,128)(2,1)S(1)} %get-tuple-element.14.gp_ref, f32[8,128]{1,0:T(8,128)S(1)} %get-tuple-element.15.cnt_ref, ...), custom_call_target="tpu_custom_call" | custom-call | tf_op jit(solution)/shard_map/attention/pallas_call | solution.py:615
  84.8 29.3 %reduce.1 = (bf16[4,96,384]{2,1,0:T(8,128)(2,1)S(1)}, bf16[2,192,384]{2,1,0:T(8,128)(2,1)S(1)}) custom-call(bf16[3072,384]{1,0:T(8,128)(2,1)S(1)} %get-tuple-element.16.g_ref, f32[384,384]{1,0:T(8,128)S(1)} %get-tuple-element.17.gq_ref, bf16[192,384]{1,0:T(8,128)(2,1)S(1)} %get-tuple-element.18.w_ref), custom_call_target="tpu_custom_call" | custom-call | tf_op jit(solution)/shard_map/reduce/pallas_call | solution.py:641
  114.2 0.0 copy-done.1
  114.2 1.8 %final.1 = (bf16[192,2,192]{2,1,0:T(2,128)(2,1)}, f32[192,192]{1,0:T(8,128)}, f32[192,192]{1,0:T(8,128)}, f32[192,192]{1,0:T(8,128)}, f32[192,192]{1,0:T(8,128)}) custom-call(bf16[4,96,384]{2,1,0:T(8,128)(2,1)S(1)} %get-tuple-element.19.ret_ref, bf16[2,192,384]{2,1,0:T(8,128)(2,1)S(1)} %get-tuple-element.20.wf_ref, bf16[192,2,192]{2,1,0:T(2,128)(2,1)S(1)} %copy-done.1), custom_call_target="tpu_custom_call" | custom-call | tf_op jit(solution)/shard_map/final/pallas_call | solution.py:661
Async XLA Ops:
  0.6 0.9 copy-start
  1.6 0.9 copy-start.2
  2.5 0.7 copy-start.7
  27.8 0.9 copy-start.3
  28.7 0.9 copy-start.4
  29.6 0.9 copy-start.5
  30.5 0.9 copy-start.6
  31.4 82.8 %copy-start.1 = (bf16[192,2,192]{2,1,0:T(2,128)(2,1)S(1)}, bf16[192,2,192]{2,1,0:T(2,128)(2,1)}, u32[]{:S(2)}) copy-start(bf16[192,2,192]{2,1,0:T(2,128)(2,1)} %grad_ref.3) | copy-start | bytes 442372

commit v3 on v2

--- a/solution.py
+++ b/solution.py
@@ -74,8 +74,7 @@
     pltpu.make_async_copy(ref, ref, sem).wait()
 
 
-def share_kernel(cells_ref, grad_ref, flag_ref, pk_ref, gp_ref, cnt_ref,
-                 cs, gs, cb, zb, s1, r1, s2, r2, zs, zr, fs, fr, ts, tr, ns, nr, ms, mr):
+def share_kernel(in_ref, pk_ref, gp_ref, cnt_ref, cs, gs, cb, zb, s1, r1, s2, r2, zs, zr, fs, fr, ts, tr, ns, nr, ms, mr):
     z, x, yl, yh, c = place()
     mine = x // 2 == c
     own = jnp.where(mine, 1, 0)
@@ -106,21 +105,13 @@
     sort = by_feature()
     left, right = shifted((ROWS, 2 * E), 0), shifted((ROWS, 2 * E), E)
 
-    def pack(ref, out):
-        rows = dot(sort, ref[...].reshape(2 * ROWS, E)).astype(BF)
+    def pack(first, out):
+        rows = dot(sort, in_ref[first:first + ROWS].reshape(2 * ROWS, E)).astype(BF)
         for f in range(2):
             r = f * ROWS
             out[f] = (dot(rows[r:r + HALF], left) + dot(rows[r + HALF:r + ROWS], right)).astype(BF)
 
-    pack(cells_ref, cs)
-    pack(grad_ref, gs)
-
-    def add(n, total):
-        return total + flag_ref[n]
-
-    flags = lax.fori_loop(0, ROWS, add, jnp.int32(0), unroll=16)
-    cb[i8] = jnp.full((8, 128), flags.astype(F32), F32)
-
+    pack(0, cs)
     pl.semaphore_wait(barrier, 4 - own + 3 + 7 + 3)
 
     my_rows = pl.ds(pl.multiple_of(((z * 4 + x) * 2 + yl) * HALF, HALF), HALF)
@@ -143,6 +134,9 @@
         def _():
             first(j)[0].start()
 
+    flags = jnp.sum(in_ref[2 * ROWS, 0:1, :].astype(F32), axis=1, keepdims=True)
+    cb[i8] = jnp.broadcast_to(flags, (8, 128))
+
     def plane(n):
         return rcopy(cb.at[i8], cb.at[i8], ns.at[n], nr.at[i8], dev8((i8 + n) % 8))
 
@@ -165,14 +159,15 @@
         copy.start()
         sent.append(copy)
 
+    for n in range(1, 8):
+        go(plane(n))
     for s in range(4):
         landed(z, c, s, r1.at[s])
         go(move(z, s, zs.at[s], zr.at[s], up))
         go(move(z, s, zs.at[4 + s], zr.at[4 + s], down))
         go(move(z, s, ts.at[s], tr.at[s], twin))
 
-    for n in range(1, 8):
-        go(plane(n))
+    pack(ROWS, gs)
     for j in range(4):
         keep = jnp.logical_and(mine, slot == j)
 
@@ -230,9 +225,8 @@
             b.wait_send()
 
 
-def attention_kernel(pk_ref, gp_ref, cnt_ref, wq_ref, wk_ref, wv_ref, wo_ref, g_ref, gq_ref, w_ref,
-                     e_ref, mb_ref, kv_ref, kT_ref, vT_ref, pT_ref, qT_ref, gT_ref, qm_ref, gm_ref,
-                     qmT_ref, gmT_ref, acc_ref, m_ref, dkv_acc, dkv_ref, attT_ref, dqT_ref, wacc_ref,
+def attention_kernel(pk_ref, gp_ref, cnt_ref, weights, g_ref, gq_ref, w_ref, e_ref, mb_ref, kv_ref, qT_ref, gT_ref, qm_ref, gm_ref,
+                     qmT_ref, gmT_ref, acc_ref, m_ref, s_ref, dkv_ref, attT_ref, dqT_ref, wacc_ref,
                      wkva, wkvb, wqa, wqb, wga, wgb, ua, ub):
     z, x, yl, yh, c = place()
     train = jnp.max(cnt_ref[...]).astype(jnp.int32)
@@ -250,10 +244,10 @@
 
     i, j = iotas((E, 128))
     heads = ones_where((i == j + HALF * yl) & (j < HALF))
-    wq = dot(wq_ref[...], heads).astype(BF)
-    wk = dot(wk_ref[...], heads).astype(BF)
-    wv = dot(wv_ref[...], heads).astype(BF)
-    wo = t_dot(wo_ref[...], heads).astype(BF)
+    wq = dot(weights[0:192, :], heads).astype(BF)
+    wk = dot(weights[192:384, :], heads).astype(BF)
+    wv = dot(weights[384:576, :], heads).astype(BF)
+    wo = t_dot(weights[576:768, :], heads).astype(BF)
     for a, b, w in ((wkva, wkvb, jnp.concatenate([wk, wv], 1)), (wqa, wqb, wq), (wga, wgb, wo)):
         a[0:192, :] = w
         a[192:256, :] = jnp.zeros((64, w.shape[1]), BF)
@@ -272,17 +266,12 @@
     @pl.loop(0, nk)
     def _(n):
         p = pk_ref[packs(n), :]
-        pT_ref[:, packs(n)] = p.T
         for h, (part, w) in enumerate(((p[:, 0:256], wkva), (p[:, 128:384], wkvb))):
             kv = dot(part, w[...])
             bias = jnp.where((lane == HALF) & (real + (n * KC + HALF * h) >= train), BIAS, 0.0)
             r = pl.ds(pl.multiple_of(n * KC + PC * h, PC), PC)
-            k = (kv[:, 0:128] + bias).astype(BF)
-            v = (kv[:, 128:256] + v_extra).astype(BF)
-            kv_ref[r, 0:128] = k
-            kv_ref[r, 128:256] = v
-            kT_ref[:, r] = k.T
-            vT_ref[:, r] = v.T
+            kv_ref[r, 0:128] = (kv[:, 0:128] + bias).astype(BF)
+            kv_ref[r, 128:256] = (kv[:, 128:256] + v_extra).astype(BF)
 
     block = z * 2 + c
     po = pk_ref[packs(block), :]
@@ -294,66 +283,88 @@
     dqT_ref[...] = jnp.zeros_like(dqT_ref)
     wacc_ref[...] = jnp.zeros_like(wacc_ref)
     i16 = lax.broadcasted_iota(jnp.int32, (16, NQ), 0)
-
-    for h in range(3):
-        hs = slice(32 * h, 32 * h + 32)
-        qmT_ref[...] = jnp.zeros_like(qmT_ref)
-        qmT_ref[hs, :] = qT_ref[hs, :]
-        qm_ref[...] = qmT_ref[...].T
-        qmT_ref[96:112, :] = jnp.where(i16 == 0, 1.0, 0.0).astype(BF)
-        acc_ref[...] = jnp.zeros_like(acc_ref)
-        m_ref[...] = jnp.full_like(m_ref, BIAS)
-
-        @pl.loop(0, nk)
-        def _(n):
-            r = rows(n)
-            vt = jnp.concatenate([vT_ref[hs, r], vT_ref[96:112, r]], 0)
-            s = dot(kv_ref[r, 0:128], qmT_ref[...]) * SCALE_LOG2E
-            old = m_ref[0:1, :]
-            new = jnp.maximum(old, jnp.ceil(jnp.max(s, axis=0, keepdims=True)))
-            e = jnp.exp2(s - new).astype(BF)
-            e_ref[r, :] = e
-            m_ref[0:1, :] = new
-            mb_ref[n, 0:1, :] = new
-            acc_ref[...] = acc_ref[...] * jnp.exp2(old - new) + dot(vt, e)
-
-        inv = 1.0 / acc_ref[32:33, :]
-        att = (acc_ref[0:32, :] * inv).astype(BF)
+    lanes = [slice(NQ * h, NQ * h + NQ) for h in range(3)]
+    subs = [slice(32 * h, 32 * h + 32) for h in range(3)]
+
+    qmT_ref[...] = jnp.zeros_like(qmT_ref)
+    gmT_ref[...] = jnp.zeros_like(gmT_ref)
+    for q, hs in zip(lanes, subs):
+        qmT_ref[hs, q] = qT_ref[hs, :]
+        qm_ref[q, :] = qmT_ref[:, q].T
+        qmT_ref[96:112, q] = jnp.where(i16 == 0, 1.0, 0.0).astype(BF)
+    acc_ref[...] = jnp.zeros_like(acc_ref)
+    m_ref[...] = jnp.full_like(m_ref, BIAS)
+
+    def piece(n, t):
+        return pl.ds(pl.multiple_of(n * KC + (t // 3) * PC, PC), PC), lanes[t % 3]
+
+    def score(n, t):
+        r, q = piece(n, t)
+        s = dot(kv_ref[r, 0:128], qmT_ref[:, q])
+        s_ref[t % 2] = s
+        m_ref[2 + t % 2:3 + t % 2, q] = jnp.max(s, axis=0, keepdims=True)
+
+    def weigh(n, t):
+        r, q = piece(n, t)
+        old = m_ref[0:1, q]
+        new = jnp.maximum(old, jnp.ceil(m_ref[2 + t % 2:3 + t % 2, q] * SCALE_LOG2E))
+        e = jnp.exp2(s_ref[t % 2] * SCALE_LOG2E - new).astype(BF)
+        e_ref[r, q] = e
+        m_ref[0:1, q] = new
+        mb_ref[n, t // 3:t // 3 + 1, q] = new
+        vT = kv_ref[r, 128:256].T
+        vt = jnp.concatenate([vT[subs[t % 3]], vT[96:112]], 0)
+        acc_ref[:, q] = acc_ref[:, q] * jnp.exp2(old - new) + dot(vt, e)
+
+    score(0, 0)
+
+    @pl.loop(0, nk)
+    def _(n):
+        for t in range(6):
+            if t < 5:
+                score(n, t + 1)
+            else:
+                score(jnp.minimum(n + 1, nk - 1), 0)
+            weigh(n, t)
+
+    for q, hs in zip(lanes, subs):
+        inv = 1.0 / acc_ref[32:33, q]
+        att = (acc_ref[0:32, q] * inv).astype(BF)
         attT_ref[hs, :] = att
         gp = (gT_ref[hs, :].astype(F32) * inv).astype(BF)
         delta = -jnp.sum(gp.astype(F32) * att.astype(F32), axis=0, keepdims=True)
         d0 = delta.astype(BF).astype(F32)
         d1 = (delta - d0).astype(BF).astype(F32)
         d2 = delta - d0 - d1
-        gmT_ref[...] = jnp.zeros_like(gmT_ref)
-        gmT_ref[hs, :] = gp
-        gm_ref[...] = gmT_ref[...].T
-        gmT_ref[96:112, :] = jnp.where(i16 == 0, d0, jnp.where(i16 == 1, d1, jnp.where(i16 == 2, d2, 0.0))).astype(BF)
-        acc_ref[...] = jnp.zeros_like(acc_ref)
-
-        @pl.loop(0, nk)
-        def _(n):
-            r = rows(n)
-            ga = dot(kv_ref[r, 128:256], gmT_ref[...]).astype(BF)
-            es = e_ref[r, :] * jnp.exp2(mb_ref[n, 0:1, :] - m_ref[0:1, :]).astype(BF)
+        gmT_ref[hs, q] = gp
+        gm_ref[q, :] = gmT_ref[:, q].T
+        gmT_ref[96:112, q] = jnp.where(i16 == 0, d0, jnp.where(i16 == 1, d1, jnp.where(i16 == 2, d2, 0.0))).astype(BF)
+    acc_ref[...] = jnp.zeros_like(acc_ref)
+
+    @pl.loop(0, nk)
+    def _(n):
+        r = rows(n)
+        v = kv_ref[r, 128:256]
+        kT, pT = kv_ref[r, 0:128].T, pk_ref[packs(n), :].T
+        dk, dv = jnp.zeros((KC, 128), F32), jnp.zeros((KC, 128), F32)
+        for h in range(3):
+            q = lanes[h]
+            ga = dot(v, gmT_ref[:, q]).astype(BF)
+            by = [jnp.exp2(mb_ref[n, t:t + 1, q] - m_ref[0:1, q]).astype(BF) for t in range(2)]
+            e = e_ref[r, q]
+            es = jnp.concatenate([e[0:PC] * by[0], e[PC:KC] * by[1]], 0)
             ds = es * ga
-            dv = dot(es, gm_ref[...])
-            dk = dot(ds, qm_ref[...]) * SCALE
-            acc_ref[0:32, :] += dot(kT_ref[hs, r], ds)
-            if h == 0:
-                dkv_acc[r, 0:128] = dk
-                dkv_acc[r, 128:256] = dv
-            elif h == 1:
-                dkv_acc[r, 0:128] += dk
-                dkv_acc[r, 128:256] += dv
-            else:
-                dkv_ref[:, 0:128] = (dkv_acc[r, 0:128] + dk).astype(BF)
-                dkv_ref[:, 128:256] = (dkv_acc[r, 128:256] + dv).astype(BF)
-                da, db = dkv_ref[0:PC, :], dkv_ref[PC:KC, :]
-                g_ref[packs(n), :] = (dot(da, ua[0:256, :]) + dot(db, ub[0:256, :])).astype(BF)
-                wacc_ref[...] += dot(pT_ref[0:E, packs(n)], da) + dot(pT_ref[E:2 * E, packs(n)], db)
-
-        dqT_ref[hs, :] = (acc_ref[0:32, :] * SCALE).astype(BF)
+            dv = dv + dot(es, gm_ref[q, :])
+            dk = dk + dot(ds, qm_ref[q, :])
+            acc_ref[0:32, q] += dot(kT[subs[h]], ds)
+        dkv_ref[:, 0:128] = (dk * SCALE).astype(BF)
+        dkv_ref[:, 128:256] = dv.astype(BF)
+        da, db = dkv_ref[0:PC, :], dkv_ref[PC:KC, :]
+        g_ref[packs(n), :] = (dot(da, ua[0:256, :]) + dot(db, ub[0:256, :])).astype(BF)
+        wacc_ref[...] += dot(pT[0:E], da) + dot(pT[E:2 * E], db)
+
+    for q, hs in zip(lanes, subs):
+        dqT_ref[hs, :] = (acc_ref[0:32, q] * SCALE).astype(BF)
 
     dq, at = dqT_ref[...].T, attT_ref[...].T
     gq_ref[...] = dot(dq[0:PC], ua[256:384, :]) + dot(dq[PC:NQ], ub[256:384, :])
@@ -586,7 +597,6 @@
 
 SLABS = 12
 VM = pl.BlockSpec(memory_space=pltpu.VMEM)
-SM = pl.BlockSpec(memory_space=pltpu.SMEM)
 DMA = pltpu.SemaphoreType.DMA
 
 
@@ -598,7 +608,7 @@
     return pl.pallas_call(
         share_kernel,
         out_shape=[sds((NR // 2, 384)), sds((PC, 384)), sds((8, 128), F32)],
-        in_specs=[VM, VM, SM],
+        in_specs=[VM],
         out_specs=[VM] * 3,
         scratch_shapes=[
             pltpu.VMEM((2, HALF, 384), BF), pltpu.VMEM((2, HALF, 384), BF),
@@ -607,6 +617,7 @@
             DMA((8,)), DMA((8,)), DMA((4,)), DMA((4,)),
         ],
         compiler_params=pltpu.CompilerParams(collective_id=1, has_side_effects=True, vmem_limit_bytes=24 * 2**20),
+        cost_estimate=pl.CostEstimate(flops=10**8, bytes_accessed=60 * 10**6, transcendentals=0),
         name="share",
     )(*args)
 
@@ -615,26 +626,26 @@
     return pl.pallas_call(
         attention_kernel,
         out_shape=[sds((NR // 2, 384)), sds((PC, 384), F32), sds((E, 384))],
-        in_specs=[VM] * 7,
+        in_specs=[VM] * 4,
         out_specs=[VM] * 3,
         scratch_shapes=[
-            pltpu.VMEM((NR, NQ), BF), pltpu.VMEM((BLOCKS, 8, NQ), F32), pltpu.VMEM((NR, 256), BF),
-            pltpu.VMEM((128, NR), BF), pltpu.VMEM((128, NR), BF), pltpu.VMEM((384, NR // 2), BF),
+            pltpu.VMEM((NR, 3 * NQ), BF), pltpu.VMEM((BLOCKS, 8, 3 * NQ), F32), pltpu.VMEM((NR, 256), BF),
             pltpu.VMEM((128, NQ), BF), pltpu.VMEM((128, NQ), BF),
-            pltpu.VMEM((NQ, 128), BF), pltpu.VMEM((NQ, 128), BF),
-            pltpu.VMEM((128, NQ), BF), pltpu.VMEM((128, NQ), BF),
-            pltpu.VMEM((48, NQ), F32), pltpu.VMEM((8, NQ), F32),
-            pltpu.VMEM((NR, 256), F32), pltpu.VMEM((KC, 256), BF),
+            pltpu.VMEM((3 * NQ, 128), BF), pltpu.VMEM((3 * NQ, 128), BF),
+            pltpu.VMEM((128, 3 * NQ), BF), pltpu.VMEM((128, 3 * NQ), BF),
+            pltpu.VMEM((48, 3 * NQ), F32), pltpu.VMEM((8, 3 * NQ), F32),
+            pltpu.VMEM((2, PC, NQ), F32), pltpu.VMEM((KC, 256), BF),
             pltpu.VMEM((128, NQ), BF), pltpu.VMEM((128, NQ), BF), pltpu.VMEM((E, 256), F32),
             pltpu.VMEM((256, 256), BF), pltpu.VMEM((256, 256), BF), pltpu.VMEM((256, 128), BF), pltpu.VMEM((256, 128), BF),
             pltpu.VMEM((256, 128), BF), pltpu.VMEM((256, 128), BF), pltpu.VMEM((384, 384), BF), pltpu.VMEM((384, 384), BF),
         ],
         compiler_params=pltpu.CompilerParams(vmem_limit_bytes=VLIM * 2**20),
+        cost_estimate=pl.CostEstimate(flops=3 * 10**10, bytes_accessed=10**7, transcendentals=14 * 10**6),
         name="attention",
     )(*args)
 
 
-VLIM = 46
+VLIM = 48
 
 
 def reduce(*args):
@@ -652,6 +663,7 @@
             DMA((16,)), DMA((16,)), DMA((8,)), DMA((8,)), DMA((16,)), DMA((16,)),
         ],
         compiler_params=pltpu.CompilerParams(collective_id=2, has_side_effects=True, vmem_limit_bytes=24 * 2**20),
+        cost_estimate=pl.CostEstimate(flops=10**8, bytes_accessed=60 * 10**6, transcendentals=0),
         name="reduce",
     )(*args)
 
@@ -669,8 +681,9 @@
 
 
 def body(cells, w_query, w_key, w_value, w_out, train_flag, grad_out):
-    packs, grads, count = share(cells, grad_out, train_flag)
-    g, gq, w = attention(packs, grads, count, w_query, w_key, w_value, w_out)
+    flags = jnp.broadcast_to(train_flag.astype(BF), (1, 2, ROWS))
+    packs, grads, count = share(jnp.concatenate([cells, grad_out, flags], 0))
+    g, gq, w = attention(packs, grads, count, jnp.concatenate([w_query, w_key, w_value, w_out], 0))
     ret, wf = reduce(g, gq, w)
     return final(ret, wf, grad_out)
 

time: 116 us -> 111 us (0.957)
  local copies, waits for them, and re-layouts: 6.09 us -> 0.01 us
  other arithmetic: 0 us -> 3.42 us
  Pallas kernels: 109 us -> 106 us
    unnamed x16 -> x2, local copies, waits for them, and re-layouts: 6.09 us -> 0.01 us
    concatenate x0 -> x2, other arithmetic: none -> 2.73 us  [the longest x1 1.63 us: body(): packs, grads, count = share(jnp.concatenate([cells, grad_out, flags], 0))]
    pallas_call x1, Pallas kernels: 53.4 us -> 51.1 us  [attention(): pl.pallas_call(attention_kernel, out_shape=[sds((NR // 2, 384)), sds((PC,...]
where the time goes in v3:
time: 111 us
  Pallas kernels  106 us (95%)
  other arithmetic  3.42 us (3%)
    pallas_call x1, Pallas kernels, attention(): pl.pallas_call(attention_kernel, out_shape=[sds((NR // 2, 384)), sds((PC,...  51.1 us
    pallas_call x1, Pallas kernels, reduce(): pl.pallas_call(reduce_kernel, out_shape=[sds((4, HALF, 384)), sds((2, E,...  29.1 us
    pallas_call x1, Pallas kernels, share(): pl.pallas_call(share_kernel, out_shape=[sds((NR // 2, 384)), sds((PC, 384...  24.4 us

profile of v3, /device:TPU:25, one launch (start us, length us, event | category | flops | bytes accessed | tf_op | source)
XLA Modules:
  0.0 110.5 jit_solution(5430964062704968039)
XLA Ops:
  0.6 0.7 convert_element_type.3
  1.3 1.6 %pad_maximum_fusion.in_ref = bf16[385,2,192]{2,1,0:T(2,128)(2,1)S(1)} fusion(bf16[1,2,192]{2,1,0:T(2,128)(2,1)S(1)} %broadcast_in_dim.3, bf16[192,2,192]{2,1,0:T(2,128)(2,1)} %grad_ref.1, bf16[192,2,192]{2,1,0:T(2,128)(2,1)} %param.7), kind=kLoop, calls=%fused_computation | loop fusion | flops 295680 | bytes 591360 | tf_op jit(solution)/shard_map/concatenate | solution.py:685
  3.0 1.1 pad_maximum_fusion.1.weights
  4.1 24.4 %share.1 = (bf16[3072,384]{1,0:T(8,128)(2,1)S(1)}, bf16[384,384]{1,0:T(8,128)(2,1)S(1)}, f32[8,128]{1,0:T(8,128)S(1)}) custom-call(bf16[385,2,192]{2,1,0:T(2,128)(2,1)S(1)} %pad_maximum_fusion.in_ref), custom_call_target="tpu_custom_call" | custom-call | flops 100000000 | bytes 60000000 | tf_op jit(solution)/shard_map/share/pallas_call | solution.py:608
  28.4 51.1 %attention.1 = (bf16[3072,384]{1,0:T(8,128)(2,1)S(1)}, f32[384,384]{1,0:T(8,128)S(1)}, bf16[192,384]{1,0:T(8,128)(2,1)S(1)}) custom-call(bf16[3072,384]{1,0:T(8,128)(2,1)S(1)} %get-tuple-element.13.pk_ref, bf16[384,384]{1,0:T(8,128)(2,1)S(1)} %get-tuple-element.14.gp_ref, f32[8,128]{1,0:T(8,128)S(1)} %get-tuple-element.15.cnt_ref, ...), custom_call_target="tpu_custom_call" | custom-call | flops 30000001024 | bytes 10000000 | tf_op jit(solution)/shard_map/attention/pallas_call | solution.py:626
  79.5 0.0 copy-start
  79.6 29.1 %reduce.1 = (bf16[4,96,384]{2,1,0:T(8,128)(2,1)S(1)}, bf16[2,192,384]{2,1,0:T(8,128)(2,1)S(1)}) custom-call(bf16[3072,384]{1,0:T(8,128)(2,1)S(1)} %get-tuple-element.16.g_ref, f32[384,384]{1,0:T(8,128)S(1)} %get-tuple-element.17.gq_ref, bf16[192,384]{1,0:T(8,128)(2,1)S(1)} %get-tuple-element.18.w_ref), custom_call_target="tpu_custom_call" | custom-call | flops 100000000 | bytes 60000000 | tf_op jit(solution)/shard_map/reduce/pallas_call | solution.py:652
  108.7 0.0 copy-done
  108.7 1.8 %final.1 = (bf16[192,2,192]{2,1,0:T(2,128)(2,1)}, f32[192,192]{1,0:T(8,128)}, f32[192,192]{1,0:T(8,128)}, f32[192,192]{1,0:T(8,128)}, f32[192,192]{1,0:T(8,128)}) custom-call(bf16[4,96,384]{2,1,0:T(8,128)(2,1)S(1)} %get-tuple-element.19.ret_ref, bf16[2,192,384]{2,1,0:T(8,128)(2,1)S(1)} %get-tuple-element.20.wf_ref, bf16[192,2,192]{2,1,0:T(2,128)(2,1)S(1)} %copy-done), custom_call_target="tpu_custom_call" | custom-call | tf_op jit(solution)/shard_map/final/pallas_call | solution.py:673
  (1 shorter events, 0.0 us)
Async XLA Ops:
  79.5 29.2 %copy-start = (bf16[192,2,192]{2,1,0:T(2,128)(2,1)S(1)}, bf16[192,2,192]{2,1,0:T(2,128)(2,1)}, u32[]{:S(2)}) copy-start(bf16[192,2,192]{2,1,0:T(2,128)(2,1)} %grad_ref.1) | copy-start | bytes 442372

commit v4 on v3

--- a/solution.py
+++ b/solution.py
@@ -74,17 +74,14 @@
     pltpu.make_async_copy(ref, ref, sem).wait()
 
 
-def share_kernel(in_ref, pk_ref, gp_ref, cnt_ref, cs, gs, cb, zb, s1, r1, s2, r2, zs, zr, fs, fr, ts, tr, ns, nr, ms, mr):
+def share_kernel(in_ref, pk_ref, gp_ref, cnt_ref, cs, gs, cf, cb, four, zb, s1, r1, s2, r2, zs, zr, fs, fr, ts, tr, ns, nr, ms, mr):
     z, x, yl, yh, c = place()
     mine = x // 2 == c
     own = jnp.where(mine, 1, 0)
     zp, zo, zn = (z + 1) % 4, (z + 2) % 4, (z + 3) % 4
     up, down, twin = device(zp, x, yl, yh, c), device(zn, x, yl, yh, c), device(z, x, yl, yh, 1 - c)
+    far = device(zo, x, yl, yh, c)
     slot = (x % 2) * 2 + yl
-    i8 = x * 2 + yl
-
-    def dev8(n):
-        return device(z, n // 2, n % 2, yh, c)
 
     barrier = pltpu.get_barrier_semaphore()
 
@@ -97,10 +94,7 @@
             greet(device(z, 2 * c + s // 2, s % 2, yh, x // 2))
     for to in (up, down, twin):
         greet(to)
-    for n in range(1, 8):
-        greet(dev8((i8 + n) % 8))
-    for n in range(1, 4):
-        greet(device((z + n) % 4, x, yl, yh, c))
+    greet(far)
 
     sort = by_feature()
     left, right = shifted((ROWS, 2 * E), 0), shifted((ROWS, 2 * E), E)
@@ -111,8 +105,10 @@
             r = f * ROWS
             out[f] = (dot(rows[r:r + HALF], left) + dot(rows[r + HALF:r + ROWS], right)).astype(BF)
 
+    flags = jnp.sum(in_ref[2 * ROWS, 0:1, :].astype(F32), axis=1, keepdims=True)
+    cf[...] = jnp.broadcast_to(flags, (8, 128))
     pack(0, cs)
-    pl.semaphore_wait(barrier, 4 - own + 3 + 7 + 3)
+    pl.semaphore_wait(barrier, 4 - own + 4)
 
     my_rows = pl.ds(pl.multiple_of(((z * 4 + x) * 2 + yl) * HALF, HALF), HALF)
     my_slot = pl.ds(pl.multiple_of(slot * HALF, HALF), HALF)
@@ -134,14 +130,19 @@
         def _():
             first(j)[0].start()
 
-    flags = jnp.sum(in_ref[2 * ROWS, 0:1, :].astype(F32), axis=1, keepdims=True)
-    cb[i8] = jnp.broadcast_to(flags, (8, 128))
-
-    def plane(n):
-        return rcopy(cb.at[i8], cb.at[i8], ns.at[n], nr.at[i8], dev8((i8 + n) % 8))
-
-    def column(n):
-        return rcopy(zb.at[z], zb.at[z], ms.at[n], mr.at[z], device((z + n) % 4, x, yl, yh, c))
+    def count(j):
+        return rcopy(cf, cb.at[slot], ns.at[j], nr.at[slot], device(z, 2 * c + j // 2, j % 2, yh, x // 2))
+
+    for j in range(4):
+        keep = jnp.logical_and(mine, slot == j)
+
+        @pl.when(keep)
+        def _():
+            pltpu.make_async_copy(cf, cb.at[slot], nr.at[slot]).start()
+
+        @pl.when(jnp.logical_not(keep))
+        def _():
+            count(j).start()
 
     def rows_of(zz, cc, s):
         return pl.ds(pl.multiple_of((zz * 2 + cc) * PC + s * HALF, HALF), HALF)
@@ -159,14 +160,16 @@
         copy.start()
         sent.append(copy)
 
-    for n in range(1, 8):
-        go(plane(n))
     for s in range(4):
         landed(z, c, s, r1.at[s])
         go(move(z, s, zs.at[s], zr.at[s], up))
         go(move(z, s, zs.at[4 + s], zr.at[4 + s], down))
         go(move(z, s, ts.at[s], tr.at[s], twin))
 
+    for s in range(4):
+        wait_for(cb.at[s], nr.at[s])
+    four[0] = cb[0] + cb[1] + cb[2] + cb[3]
+    go(rcopy(four.at[0], four.at[1], ms.at[0], mr.at[0], twin))
     pack(ROWS, gs)
     for j in range(4):
         keep = jnp.logical_and(mine, slot == j)
@@ -178,6 +181,11 @@
         @pl.when(jnp.logical_not(keep))
         def _():
             first(j)[1].start()
+
+    wait_for(four.at[1], mr.at[0])
+    zb[0] = four[0] + four[1]
+    for n, to in ((1, up), (2, far), (3, down)):
+        go(rcopy(zb.at[0], zb.at[n], ms.at[n], mr.at[n], to))
 
     for i in range(4):
         s = i
@@ -191,23 +199,12 @@
             go(move(zp, s, fs.at[s], fr.at[s], down))
         go(move(zp, s, ts.at[8 + s], tr.at[8 + s], twin))
 
-    for n in range(1, 8):
-        m = (i8 + n) % 8
-        wait_for(cb.at[m], nr.at[m])
-    total = cb[0]
-    for n in range(1, 8):
-        total = total + cb[n]
-    zb[z] = total
-    for n in range(1, 4):
-        go(column(n))
-
     for s in (0, 2, 1, 3):
         landed(zo, c, s, fr.at[s])
         go(move(zo, s, ts.at[12 + s], tr.at[12 + s], twin))
 
     for n in range(1, 4):
-        m = (z + n) % 4
-        wait_for(zb.at[m], mr.at[m])
+        wait_for(zb.at[n], mr.at[n])
     cnt_ref[...] = zb[0] + zb[1] + zb[2] + zb[3]
 
     for n, zz in ((0, z), (1, zn), (2, zp), (3, zo)):
@@ -223,6 +220,7 @@
             a, b = first(j)
             a.wait_send()
             b.wait_send()
+            count(j).wait_send()
 
 
 def attention_kernel(pk_ref, gp_ref, cnt_ref, weights, g_ref, gq_ref, w_ref, e_ref, mb_ref, kv_ref, qT_ref, gT_ref, qm_ref, gm_ref,
@@ -230,7 +228,9 @@
                      wkva, wkvb, wqa, wqb, wga, wgb, ua, ub):
     z, x, yl, yh, c = place()
     train = jnp.max(cnt_ref[...]).astype(jnp.int32)
-    nk = lax.div(train + KC - 1, KC)
+    halves = lax.div(train + PC - 1, PC)
+    full, odd = lax.div(halves, 2), lax.rem(halves, 2)
+    last = lax.div(halves - 1, 2)
 
     def rows(n):
         return pl.ds(pl.multiple_of(n * KC, KC), KC)
@@ -238,9 +238,12 @@
     def packs(n):
         return pl.ds(pl.multiple_of(n * PC, PC), PC)
 
-    @pl.loop(nk, BLOCKS)
+    def half_packs(n):
+        return pl.ds(pl.multiple_of(n * ROWS, ROWS), ROWS)
+
+    @pl.loop(halves, 2 * BLOCKS)
     def _(n):
-        g_ref[packs(n), :] = jnp.zeros((PC, 384), BF)
+        g_ref[half_packs(n), :] = jnp.zeros((ROWS, 384), BF)
 
     i, j = iotas((E, 128))
     heads = ones_where((i == j + HALF * yl) & (j < HALF))
@@ -258,20 +261,25 @@
         ua[128 * n:128 * n + 128, :] = t_dot(w, left).astype(BF)
         ub[128 * n:128 * n + 128, :] = t_dot(w, right).astype(BF)
 
-    lane = lax.broadcasted_iota(jnp.int32, (PC, 128), 1)
-    sub = lax.broadcasted_iota(jnp.int32, (PC, 128), 0)
-    real = sub + 96 * ((sub >= 96).astype(jnp.int32) + (sub >= 192).astype(jnp.int32) + (sub >= 288).astype(jnp.int32))
+    lane = lax.broadcasted_iota(jnp.int32, (ROWS, 128), 1)
+    sub = lax.broadcasted_iota(jnp.int32, (ROWS, 128), 0)
+    real = sub + HALF * (sub >= HALF).astype(jnp.int32)
     v_extra = jnp.where((lane >= HALF) & (lane < HALF + 3), 1.0, 0.0)
 
-    @pl.loop(0, nk)
-    def _(n):
+    def project(n):
         p = pk_ref[packs(n), :]
-        for h, (part, w) in enumerate(((p[:, 0:256], wkva), (p[:, 128:384], wkvb))):
-            kv = dot(part, w[...])
-            bias = jnp.where((lane == HALF) & (real + (n * KC + HALF * h) >= train), BIAS, 0.0)
-            r = pl.ds(pl.multiple_of(n * KC + PC * h, PC), PC)
-            kv_ref[r, 0:128] = (kv[:, 0:128] + bias).astype(BF)
-            kv_ref[r, 128:256] = (kv[:, 128:256] + v_extra).astype(BF)
+        for side, (cells, w) in enumerate(((p[:, 0:256], wkva), (p[:, 128:384], wkvb))):
+            kv = dot(cells, w[...])
+            for half in range(2):
+                first = n * KC + PC * half
+                bias = jnp.where((lane == HALF) & (real + (first + HALF * side) >= train), BIAS, 0.0)
+                r = pl.ds(pl.multiple_of(first + ROWS * side, ROWS), ROWS)
+                own = slice(ROWS * half, ROWS * half + ROWS)
+                kv_ref[r, 0:128] = (kv[own, 0:128] + bias).astype(BF)
+                kv_ref[r, 128:256] = (kv[own, 128:256] + v_extra).astype(BF)
+
+    project(0)
+    project(jnp.minimum(1, last))
 
     block = z * 2 + c
     po = pk_ref[packs(block), :]
@@ -318,14 +326,22 @@
 
     score(0, 0)
 
-    @pl.loop(0, nk)
+    @pl.loop(0, full)
     def _(n):
         for t in range(6):
             if t < 5:
                 score(n, t + 1)
             else:
-                score(jnp.minimum(n + 1, nk - 1), 0)
+                score(jnp.minimum(n + 1, last), 0)
             weigh(n, t)
+        project(jnp.minimum(n + 2, last))
+
+    @pl.when(odd == 1)
+    def _():
+        for t in range(3):
+            if t < 2:
+                score(full, t + 1)
+            weigh(full, t)
 
     for q, hs in zip(lanes, subs):
         inv = 1.0 / acc_ref[32:33, q]
@@ -341,27 +357,38 @@
         gmT_ref[96:112, q] = jnp.where(i16 == 0, d0, jnp.where(i16 == 1, d1, jnp.where(i16 == 2, d2, 0.0))).astype(BF)
     acc_ref[...] = jnp.zeros_like(acc_ref)
 
-    @pl.loop(0, nk)
-    def _(n):
-        r = rows(n)
+    def pass_two(n, many):
+        size = many * PC
+        r = pl.ds(pl.multiple_of(n * KC, KC), size)
         v = kv_ref[r, 128:256]
-        kT, pT = kv_ref[r, 0:128].T, pk_ref[packs(n), :].T
-        dk, dv = jnp.zeros((KC, 128), F32), jnp.zeros((KC, 128), F32)
+        kT = kv_ref[r, 0:128].T
+        dk, dv = jnp.zeros((size, 128), F32), jnp.zeros((size, 128), F32)
         for h in range(3):
             q = lanes[h]
             ga = dot(v, gmT_ref[:, q]).astype(BF)
-            by = [jnp.exp2(mb_ref[n, t:t + 1, q] - m_ref[0:1, q]).astype(BF) for t in range(2)]
             e = e_ref[r, q]
-            es = jnp.concatenate([e[0:PC] * by[0], e[PC:KC] * by[1]], 0)
+            by = [jnp.exp2(mb_ref[n, t:t + 1, q] - m_ref[0:1, q]).astype(BF) for t in range(many)]
+            es = jnp.concatenate([e[PC * t:PC * t + PC] * by[t] for t in range(many)], 0)
             ds = es * ga
             dv = dv + dot(es, gm_ref[q, :])
             dk = dk + dot(ds, qm_ref[q, :])
             acc_ref[0:32, q] += dot(kT[subs[h]], ds)
-        dkv_ref[:, 0:128] = (dk * SCALE).astype(BF)
-        dkv_ref[:, 128:256] = dv.astype(BF)
-        da, db = dkv_ref[0:PC, :], dkv_ref[PC:KC, :]
-        g_ref[packs(n), :] = (dot(da, ua[0:256, :]) + dot(db, ub[0:256, :])).astype(BF)
-        wacc_ref[...] += dot(pT[0:E], da) + dot(pT[E:2 * E], db)
+        dkv_ref[0:size, 0:128] = (dk * SCALE).astype(BF)
+        dkv_ref[0:size, 128:256] = dv.astype(BF)
+        for t in range(many):
+            p = half_packs(2 * n + t)
+            pT = pk_ref[p, :].T
+            da, db = dkv_ref[PC * t:PC * t + ROWS, :], dkv_ref[PC * t + ROWS:PC * t + PC, :]
+            g_ref[p, :] = (dot(da, ua[0:256, :]) + dot(db, ub[0:256, :])).astype(BF)
+            wacc_ref[...] += dot(pT[0:E], da) + dot(pT[E:2 * E], db)
+
+    @pl.loop(0, full)
+    def _(n):
+        pass_two(n, 2)
+
+    @pl.when(odd == 1)
+    def _():
+        pass_two(full, 1)
 
     for q, hs in zip(lanes, subs):
         dqT_ref[hs, :] = (acc_ref[0:32, q] * SCALE).astype(BF)
@@ -393,12 +420,6 @@
     owner = i16 < SLABS
     owns = jnp.where(owner, 1, 0)
 
-    def dev16(n):
-        return device(n // 4, n % 4, yl, yh, c)
-
-    def dev8(n):
-        return device(z, x, (n // 2) % 2, n // 4, n % 2)
-
     barrier = pltpu.get_barrier_semaphore()
 
     def greet(to):
@@ -411,13 +432,13 @@
         def _():
             greet(device(z, 2 * c + j // 2, j % 2, yh, x // 2))
 
-    @pl.loop(1, 16)
-    def _(n):
-        greet(dev16((i16 + n) % 16))
-
-    @pl.loop(1, 8)
-    def _(n):
-        greet(dev8((i8 + n) % 8))
+    zs_, xs_ = [z, zp, zo, zn], [x, (x + 1) % 4, (x + 2) % 4, (x + 3) % 4]
+    around = [(zs_[n // 4], xs_[n % 4]) for n in range(16)]
+    beside = [((yl + n // 2 % 2) % 2, (yh + n // 4) % 2, (c + n % 2) % 2) for n in range(8)]
+    for n in range(1, 16):
+        greet(device(*around[n], yl, yh, c))
+    for n in range(1, 8):
+        greet(device(z, x, *beside[n]))
 
     pl.semaphore_wait(barrier, 3 + 4 - own + 15 + 7)
 
@@ -437,18 +458,22 @@
         return pl.ds(pl.multiple_of(n * 16, 16), 16)
 
     def one(n):
-        to = (i16 + n) % 16
-        return to < SLABS, rcopy(w_ref.at[slab(jnp.minimum(to, SLABS - 1)), :], rs.at[i16], as_.at[n], ar.at[i16], dev16(to))
+        zz, xx = around[n]
+        to = zz * 4 + xx
+        ok = to < SLABS
+        r = slab(jnp.minimum(to, SLABS - 1))
+        return ok, rcopy(w_ref.at[r, :], rs.at[i16], as_.at[n], ar.at[i16], device(zz, xx, yl, yh, c))
 
     def two(n):
-        return rcopy(p2.at[i8], p2.at[i8], bs.at[n], br.at[i8], dev8((i8 + n) % 8))
+        return rcopy(p2.at[i8], p2.at[i8], bs.at[n], br.at[i8], device(z, x, *beside[n]))
+
+    my_slab = slab(jnp.minimum(i16, SLABS - 1))
 
     def three(n):
-        mine_ = slab(jnp.minimum(i16, SLABS - 1))
-        return rcopy(wf_ref.at[:, mine_, :], wf_ref.at[:, mine_, :], cs.at[n], cr.at[i16], dev16((i16 + n) % 16))
-
-    @pl.loop(1, 16)
-    def _(n):
+        mine_ = wf_ref.at[:, my_slab, :]
+        return rcopy(mine_, mine_, cs.at[n], cr.at[i16], device(*around[n], yl, yh, c))
+
+    for n in range(1, 16):
         ok, copy = one(n)
 
         @pl.when(ok)
@@ -472,9 +497,8 @@
     def _():
         rs[i16] = w_ref[slab(jnp.minimum(i16, SLABS - 1)), :]
 
-        @pl.loop(1, 16)
-        def _(n):
-            m = (i16 + n) % 16
+        for n in range(1, 16):
+            m = around[n][0] * 4 + around[n][1]
             wait_for(rs.at[m], ar.at[m])
 
         acc = rs[0].astype(F32)
@@ -482,8 +506,7 @@
             acc = acc + rs[n].astype(F32)
         p2[i8] = acc.astype(BF)
 
-        @pl.loop(1, 8)
-        def _(n):
+        for n in range(1, 8):
             two(n).start()
 
     wait_for(hp, hr.at[0])
@@ -495,9 +518,8 @@
 
     @pl.when(owner)
     def _():
-        @pl.loop(1, 8)
-        def _(n):
-            m = (i8 + n) % 8
+        for yl_, yh_, c_ in beside[1:]:
+            m = (yh_ * 2 + yl_) * 2 + c_
             wait_for(p2.at[m], br.at[m])
 
         for half in range(2):
@@ -505,8 +527,7 @@
             acc = p2[n].astype(F32) + p2[n + 1].astype(F32) + p2[n + 4].astype(F32) + p2[n + 5].astype(F32)
             wf_ref[half, slab(jnp.minimum(i16, SLABS - 1)), :] = acc.astype(BF)
 
-        @pl.loop(1, 16)
-        def _(n):
+        for n in range(1, 16):
             three(n).start()
 
     total = with_twin(3, z) + gq_ref[...]
@@ -534,9 +555,8 @@
     for n in range(4):
         wait_for(ret_ref.at[n], kr.at[n])
 
-    @pl.loop(1, 16)
-    def _(n):
-        m = (i16 + n) % 16
+    for n in range(1, 16):
+        m = around[n][0] * 4 + around[n][1]
 
         @pl.when(m < SLABS)
         def _():
@@ -550,22 +570,18 @@
         def _():
             back(s).wait_send()
 
-    @pl.loop(1, 16)
-    def _(n):
+    for n in range(1, 16):
         ok, copy = one(n)
 
         @pl.when(ok)
         def _():
             copy.wait_send()
-
-        @pl.when(owner)
-        def _():
-            three(n).wait_send()
 
     @pl.when(owner)
     def _():
-        @pl.loop(1, 8)
-        def _(n):
+        for n in range(1, 16):
+            three(n).wait_send()
+        for n in range(1, 8):
             two(n).wait_send()
 
 
@@ -612,9 +628,9 @@
         out_specs=[VM] * 3,
         scratch_shapes=[
             pltpu.VMEM((2, HALF, 384), BF), pltpu.VMEM((2, HALF, 384), BF),
-            pltpu.VMEM((8, 8, 128), F32), pltpu.VMEM((4, 8, 128), F32),
+            pltpu.VMEM((8, 128), F32), pltpu.VMEM((4, 8, 128), F32), pltpu.VMEM((2, 8, 128), F32), pltpu.VMEM((4, 8, 128), F32),
             DMA((4,)), DMA((4,)), DMA((4,)), DMA((4,)), DMA((8,)), DMA((8,)), DMA((4,)), DMA((4,)), DMA((16,)), DMA((16,)),
-            DMA((8,)), DMA((8,)), DMA((4,)), DMA((4,)),
+            DMA((4,)), DMA((4,)), DMA((4,)), DMA((4,)),
         ],
         compiler_params=pltpu.CompilerParams(collective_id=1, has_side_effects=True, vmem_limit_bytes=24 * 2**20),
         cost_estimate=pl.CostEstimate(flops=10**8, bytes_accessed=60 * 10**6, transcendentals=0),

time: 111 us -> 87.6 us (0.79)
  Pallas kernels: 106 us -> 83.3 us
    pallas_call x1, Pallas kernels: 51.1 us -> 29.2 us  [attention(): pl.pallas_call(attention_kernel, out_shape=[sds((NR // 2, 384)), sds((PC,...]
    pallas_call x1, Pallas kernels: 24.4 us -> 22.5 us  [share(): pl.pallas_call(share_kernel, out_shape=[sds((NR // 2, 384)), sds((PC, 384...]
where the time goes in v4:
time: 87.6 us; the launch traced here: 87.5 us
  Pallas kernels  83.3 us (95%)
  other arithmetic  3.42 us (4%)
    pallas_call x1, Pallas kernels, reduce(): pl.pallas_call(reduce_kernel, out_shape=[sds((4, HALF, 384)), sds((2, E,...  29.8 us
    pallas_call x1, Pallas kernels, attention(): pl.pallas_call(attention_kernel, out_shape=[sds((NR // 2, 384)), sds((PC,...  29.2 us
    pallas_call x1, Pallas kernels, share(): pl.pallas_call(share_kernel, out_shape=[sds((NR // 2, 384)), sds((PC, 384...  22.5 us
    pallas_call x1, Pallas kernels, final(): pl.pallas_call(final_kernel, out_shape=[sds((ROWS, 2, E)), w, w, w, w], i...  1.83 us

profile of v4, /device:TPU:25, one launch (start us, length us, event | category | flops | bytes accessed | tf_op | source)
XLA Modules:
  0.0 87.5 jit_solution(16974423878845469207)
XLA Ops:
  0.6 0.7 convert_element_type.3
  1.3 1.6 %pad_maximum_fusion.in_ref = bf16[385,2,192]{2,1,0:T(2,128)(2,1)S(1)} fusion(bf16[1,2,192]{2,1,0:T(2,128)(2,1)S(1)} %broadcast_in_dim.3, bf16[192,2,192]{2,1,0:T(2,128)(2,1)} %grad_ref.1, bf16[192,2,192]{2,1,0:T(2,128)(2,1)} %param.7), kind=kLoop, calls=%fused_computation | loop fusion | flops 295680 | bytes 591360 | tf_op jit(solution)/shard_map/concatenate | solution.py:701
  3.0 1.1 %pad_maximum_fusion.1.weights = bf16[768,192]{1,0:T(8,128)(2,1)S(1)} fusion(bf16[192,192]{1,0:T(8,128)(2,1)} %param.11, bf16[192,192]{1,0:T(8,128)(2,1)} %param.10, bf16[192,192]{1,0:T(8,128)(2,1)} %param.9, bf16[192,192]{1,0:T(8,128)(2,1)} %param.8), kind=kLoop, calls=%fused_computation.1 | loop fusion | flops 1179648 | bytes 589824 | tf_op jit(solution)/shard_map/concatenate | solution.py:702
  4.1 22.5 %share.1 = (bf16[3072,384]{1,0:T(8,128)(2,1)S(1)}, bf16[384,384]{1,0:T(8,128)(2,1)S(1)}, f32[8,128]{1,0:T(8,128)S(1)}) custom-call(bf16[385,2,192]{2,1,0:T(2,128)(2,1)S(1)} %pad_maximum_fusion.in_ref), custom_call_target="tpu_custom_call" | custom-call | flops 100000000 | bytes 60000000 | tf_op jit(solution)/shard_map/share/pallas_call | solution.py:624
  26.6 29.2 %attention.1 = (bf16[3072,384]{1,0:T(8,128)(2,1)S(1)}, f32[384,384]{1,0:T(8,128)S(1)}, bf16[192,384]{1,0:T(8,128)(2,1)S(1)}) custom-call(bf16[3072,384]{1,0:T(8,128)(2,1)S(1)} %get-tuple-element.13.pk_ref, bf16[384,384]{1,0:T(8,128)(2,1)S(1)} %get-tuple-element.14.gp_ref, f32[8,128]{1,0:T(8,128)S(1)} %get-tuple-element.15.cnt_ref, ...), custom_call_target="tpu_custom_call" | custom-call | flops 30000001024 | bytes 10000000 | tf_op jit(solution)/shard_map/attention/pallas_call | solution.py:642
  55.8 0.0 copy-start
  55.8 29.8 %reduce.1 = (bf16[4,96,384]{2,1,0:T(8,128)(2,1)S(1)}, bf16[2,192,384]{2,1,0:T(8,128)(2,1)S(1)}) custom-call(bf16[3072,384]{1,0:T(8,128)(2,1)S(1)} %get-tuple-element.16.g_ref, f32[384,384]{1,0:T(8,128)S(1)} %get-tuple-element.17.gq_ref, bf16[192,384]{1,0:T(8,128)(2,1)S(1)} %get-tuple-element.18.w_ref), custom_call_target="tpu_custom_call" | custom-call | flops 100000000 | bytes 60000000 | tf_op jit(solution)/shard_map/reduce/pallas_call | solution.py:668
  85.6 0.0 copy-done
  85.6 1.8 %final.1 = (bf16[192,2,192]{2,1,0:T(2,128)(2,1)}, f32[192,192]{1,0:T(8,128)}, f32[192,192]{1,0:T(8,128)}, f32[192,192]{1,0:T(8,128)}, f32[192,192]{1,0:T(8,128)}) custom-call(bf16[4,96,384]{2,1,0:T(8,128)(2,1)S(1)} %get-tuple-element.19.ret_ref, bf16[2,192,384]{2,1,0:T(8,128)(2,1)S(1)} %get-tuple-element.20.wf_ref, bf16[192,2,192]{2,1,0:T(2,128)(2,1)S(1)} %copy-done), custom_call_target="tpu_custom_call" | custom-call | tf_op jit(solution)/shard_map/final/pallas_call | solution.py:689
  (1 shorter events, 0.0 us)
Async XLA Ops:
  55.8 29.8 %copy-start = (bf16[192,2,192]{2,1,0:T(2,128)(2,1)S(1)}, bf16[192,2,192]{2,1,0:T(2,128)(2,1)}, u32[]{:S(2)}) copy-start(bf16[192,2,192]{2,1,0:T(2,128)(2,1)} %grad_ref.1) | copy-start | bytes 442372
